TPU v7x, 512 devices: a whole 4x8x8 slice. The times are simulated.
512 devices in a mesh: doc: 128 (over z, y, core), term: 4 (over x).
Axes of the slice: x: 4, y: 8, z: 8, core: 2. Of those that a mesh axis runs over, the one named last changes fastest.
Arguments:
- tf_blocks: bfloat16 [128, 8192, 512], P('doc', 'term'), as said below
- block_scale: float32 [128, 64, 4], P('doc', 'term'), may hold values from 0.3 to 3
- term_blocks: int32 [128, 64], P('doc', 'term'), may hold values from 0 to 255, as said below
- prior_rows: bfloat16 [128, 8192, 256], P('doc', 'term'), as said below
- prior_sv: float32 [256], replicated, may hold values from 0.3 to 1.5
Outputs:
- doc_coords: float32 [65536, 256], P(('doc', 'term'))
- new_rows: bfloat16 [128, 8192, 256], P('doc', 'term')
- singular: float32 [256], replicated
Inputs may be any that keep to these rules, and one draw needn't show every extreme that they name: `term_blocks`: within one batch and one index of term the 16 block ids are distinct and increasing. `prior_rows`: stored rows with the same term row are equal in every batch. `tf_blocks`: entries are nonnegative; about half are zero.
All inputs are finite; a program needn't handle non-finite values.
Results may differ from a plain program's by a relative error of at most 0.0078.
Values sent between devices are 32-bit elements; how exact they have to be, the bound alone decides.
No kernel may reach another device: no remote copies, remote signals or barrier semaphores. Data moves between devices by JAX's collectives and lax.ppermute only.
A program may use at most 64 MiB of HBM per device.

v0:
```python
import functools
import math

import jax
import jax.numpy as jnp
from jax import lax
from jax.experimental import pallas as pl
from jax.experimental.pallas import tpu as pltpu
from jax.sharding import Mesh
from jax.sharding import PartitionSpec as P

TERMS = 131072
ITERS = 4
SHARE_BLOCKS = 256
LANES = 128
PANEL = 16
OUTER = 128


forget_factor = 0.85
highest = lax.Precision.HIGHEST


def contract(a, b, a_dim, b_dim):
    return lax.dot_general(
        a,
        b,
        (((a_dim,), (b_dim,)), ((), ())),
        precision=highest,
        preferred_element_type=jnp.float32,
    )


def eliminate(panel, first):
    size = panel.shape[0]
    rows = lax.broadcasted_iota(jnp.int32, (size, LANES), 0)
    columns = [
        jnp.broadcast_to(panel[:, first + k : first + k + 1], (size, LANES)) for k in range(size)
    ]
    tiles = [panel[:, t : t + LANES] for t in range(0, panel.shape[1], LANES)]
    pivots = jnp.zeros((size, LANES), jnp.float32)
    for k in range(size):
        pivot = columns[k][k : k + 1, :]
        pivots = jnp.where(rows == k, jnp.broadcast_to(pivot, (size, LANES)), pivots)
        if k + 1 < size:
            factor = jnp.where(rows > k, columns[k] * (1.0 / pivot), 0.0)
            for m in range(k + 1, size):
                columns[m] = columns[m] - factor * columns[m][k : k + 1, :]
            tiles = [tile - factor * tile[k : k + 1, :] for tile in tiles]
    root = lax.rsqrt(pivots)
    return jnp.concatenate([tile * root for tile in tiles], axis=1)


def orthonormal_rows(work):
    size = work.shape[0]
    for outer in range(0, size, OUTER):
        end = outer + OUTER
        for first in range(outer, end, PANEL):
            panel = work[first : first + PANEL, :]
            if first > outer:
                panel = panel - contract(
                    work[outer:first, first : first + PANEL], work[outer:first, :], 0, 0
                )
            work[first : first + PANEL, :] = eliminate(panel, first)
        if end < size:
            work[end:, :] = work[end:, :] - contract(work[outer:end, end:size], work[outer:end, :], 0, 0)


def iterate(window_ref, sv_ref, rotation_ref, singular_ref, gram, work):
    size = window_ref.shape[0]
    row = lax.broadcasted_iota(jnp.int32, (size, size), 0)
    column = lax.broadcasted_iota(jnp.int32, (size, size), 1)
    sv = sv_ref[...]
    gram[...] = window_ref[...] + jnp.where(row == column, forget_factor * sv * sv, 0.0)
    work[:, size:] = gram[...]

    def step(iteration, carry):
        image = work[:, size:]
        work[:, :size] = contract(image, image, 1, 1)
        orthonormal_rows(work)
        rotation_ref[...] = work[:, size:]
        work[:, size:] = contract(rotation_ref[...], gram[...], 1, 0)
        return carry

    lax.fori_loop(0, ITERS, step, 0)
    singular_ref[...] = jnp.sqrt(
        jnp.sum(rotation_ref[...] * work[:, size:], axis=1, keepdims=True)
    )


def all_to_all(pieces, axes):
    return lax.all_to_all(pieces, axes, 0, 0, tiled=True)


def repeat(piece, count):
    return jnp.broadcast_to(piece[None], (count,) + piece.shape)


def swap_cores(array):
    return lax.ppermute(array, "core", [(0, 1), (1, 0)])


def split_cores(array):
    half = array.shape[0] // 2
    first = lax.axis_index("core") == 0
    low, high = array[:half], array[half:]
    return jnp.where(first, low, high) + swap_cores(jnp.where(first, high, low))


def join_cores(half):
    other = swap_cores(half)
    first = lax.axis_index("core") == 0
    return jnp.concatenate([jnp.where(first, half, other), jnp.where(first, other, half)], axis=0)


def shards(tf_blocks, block_scale, term_blocks, prior_rows, prior_sv):
    counts = tf_blocks[0]
    scales = block_scale[0]
    block_ids = term_blocks[0]
    basis_rows = prior_rows[0]
    stored_blocks = block_ids.shape[0]
    height = counts.shape[0]
    block_width = height // stored_blocks
    batch_docs = counts.shape[1]
    doc_blocks = batch_docs // block_width
    rank_size = basis_rows.shape[1]
    planes, lines = lax.axis_size("z"), lax.axis_size("y")
    doc_count = planes * lines * lax.axis_size("core")
    term_count = lax.axis_size("term")
    total_docs = batch_docs * doc_count
    share_docs = batch_docs // term_count
    marker = (
        jnp.arange(batch_docs, dtype=jnp.int32)[:, None] // block_width
        == jnp.arange(doc_blocks, dtype=jnp.int32)[None, :]
    ).astype(jnp.bfloat16)
    block_sums = jnp.dot(counts, marker, preferred_element_type=jnp.float32)
    scale_rows = jnp.repeat(scales, block_width, axis=0)
    row_mass = jnp.sum(block_sums * scale_rows, axis=1).reshape(stored_blocks, block_width)
    places = (
        block_ids[:, None] == jnp.arange(SHARE_BLOCKS, dtype=jnp.int32)[None, :]
    ).astype(jnp.float32)
    dense = jnp.dot(places.T, row_mass, precision=highest)
    chips = ("z", "y")
    chip_count = planes * lines
    half_mass = split_cores(dense).reshape(chip_count, -1, block_width)
    own_mass = jnp.sum(all_to_all(half_mass, chips), axis=0)
    half_mass = all_to_all(repeat(own_mass, chip_count), chips).reshape(-1, block_width)
    share_mass = join_cores(half_mass)
    term_mass = jnp.dot(places, share_mass, precision=highest)
    weight = jnp.log(1.0 + total_docs / (1.0 + term_mass)).reshape(height)
    root_terms = math.sqrt(TERMS)
    pieces = []
    for column in range(doc_blocks):
        basis_half = (
            basis_rows * (weight * scale_rows[:, column] / root_terms)[:, None]
        ).astype(jnp.bfloat16)
        doc_block = counts[:, column * block_width : (column + 1) * block_width]
        pieces.append(
            lax.dot_general(
                doc_block, basis_half, (((0,), (0,)), ((), ())), preferred_element_type=jnp.float32
            )
        )
    partial = jnp.concatenate(pieces, axis=0).reshape(term_count, share_docs, rank_size)
    share_rows = jnp.sum(all_to_all(partial, "term"), axis=0)
    own_gram = jnp.dot(share_rows.T, share_rows, precision=highest) / total_docs
    flat_gram = jnp.concatenate([own_gram[:, t : t + LANES] for t in range(0, rank_size, LANES)])
    plane = ("y", "term")
    plane_count = lines * term_count
    half_gram = split_cores(flat_gram).reshape(plane_count, -1, LANES)
    plane_gram = jnp.sum(all_to_all(half_gram, plane), axis=0)
    piece_gram = jnp.sum(all_to_all(repeat(plane_gram, planes), "z"), axis=0)
    half_gram = all_to_all(repeat(piece_gram, plane_count), plane).reshape(-1, LANES)
    flat_gram = join_cores(half_gram)
    window = jnp.concatenate(
        [flat_gram[t : t + rank_size] for t in range(0, flat_gram.shape[0], rank_size)], axis=1
    )
    rotation, singular = pl.pallas_call(
        iterate,
        out_shape=(
            jax.ShapeDtypeStruct((rank_size, rank_size), jnp.float32),
            jax.ShapeDtypeStruct((rank_size, 1), jnp.float32),
        ),
        scratch_shapes=[
            pltpu.VMEM((rank_size, rank_size), jnp.float32),
            pltpu.VMEM((rank_size, 2 * rank_size), jnp.float32),
        ],
        compiler_params=pltpu.CompilerParams(vmem_limit_bytes=32 * 2**20),
    )(window, prior_sv.reshape(1, rank_size))
    doc_coords = contract(share_rows, rotation, 1, 1)
    rotation_half = rotation.astype(jnp.bfloat16)
    new_rows = lax.dot_general(
        basis_rows, rotation_half, (((1,), (1,)), ((), ())), preferred_element_type=jnp.float32
    ).astype(jnp.bfloat16)
    return (doc_coords, new_rows[None], singular.reshape(rank_size))


def solution(mesh):
    planes = lines = 8
    named = Mesh(
        mesh.devices.reshape(planes, lines, -1, mesh.shape["term"]), ("z", "y", "core", "term")
    )
    doc = ("z", "y", "core")
    in_specs = (
        P(doc, "term", None),
        P(doc, "term", None),
        P(doc, "term"),
        P(doc, "term", None),
        P(),
    )
    out_specs = (P(doc + ("term",), None), P(doc, "term", None), P())
    return jax.shard_map(shards, mesh=named, in_specs=in_specs, out_specs=out_specs, check_vma=False)
```

profile of v0, /device:TPU:1, one launch (start us, length us, event | category | flops | bytes accessed | tf_op | source)
XLA Modules:
  0.0 162.5 jit_solution(4800280742507956904)
XLA Ops:
  0.6 0.0 copy-start
  0.6 0.0 copy-start.2
  0.7 0.0 copy-start.4
  0.7 0.0 copy-start.3
  0.7 0.6 copy-done
  1.3 0.1 broadcast_bitcast_fusion
  1.4 2.6 %fusion.6 = f32[2048]{0:T(1024)S(1)} fusion(s32[512]{0:T(512)S(1)} %add_select_fusion, bf16[1,2048,512]{2,1,0:T(8,128)(2,1)} %param.5, f32[1,4,16,128]{3,2,1,0:T(8,128)S(1)} %broadcast_bitcast_fusion), kind=kOutput, calls=%fused_computation.17 | convolution fusion | flops 8407040 | bytes 2140160 | tf_op jit(solution)/shard_map/dot_general | solution.py:136
  4.0 0.0 copy-done.4
  4.0 0.4 fusion.34
  4.4 8.8 %collective-permute-start = (f32[128,128]{1,0:T(8,128)S(1)}, f32[128,128]{1,0:T(8,128)S(1)}, u32[]{:S(2)}, u32[]{:S(2)}) collective-permute-start(f32[128,128]{1,0:T(8,128)S(1)} %slice_select_fusion.1), channel_id=1, source_target_pairs={{0,4},{4,0},{1,5},{5,1},{2,6},{6,2},{3,7},{7,3},{8,12},{12,8},{9,1... | collective-permute-start | bytes 196616 | tf_op jit(solution)/shard_map/ppermute | solution.py:100
  13.2 0.9 collective-permute-done
  14.1 21.8 %all_to_all.30 = f32[64,2,128]{2,1,0:T(2,128)S(1)} all-to-all(f32[64,2,128]{2,1,0:T(2,128)S(1)} %bitcast.82), channel_id=1, replica_groups=mesh['z'=8,'y'=8,'core'=2,'term'=4] {'z','y'}, dimensions={0} | all-to-all | bytes 131072 | tf_op jit(solution)/shard_map/all_to_all | solution.py:92
  35.9 0.1 reduce_sum.46
  36.0 14.9 %all_to_all.31 = f32[64,2,128]{2,1,0:T(2,128)S(1)} all-to-all(f32[64,2,128]{2,1,0:T(2,128)S(1)} %broadcast_in_dim.11), channel_id=1, replica_groups=mesh['z'=8,'y'=8,'core'=2,'term'=4] {'z','y'}, dimensions={0} | all-to-all | bytes 131072 | tf_op jit(solution)/shard_map/all_to_all | solution.py:92
  50.9 4.8 %collective-permute-start.1 = (f32[128,128]{1,0:T(8,128)S(1)}, f32[128,128]{1,0:T(8,128)S(1)}, u32[]{:S(2)}, u32[]{:S(2)}) collective-permute-start(f32[128,128]{1,0:T(8,128)S(1)} %bitcast.80), channel_id=1, source_target_pairs={{0,4},{4,0},{1,5},{5,1},{2,6},{6,2},{3,7},{7,3},{8,12},{12,8},{9,1... | collective-permute-start | bytes 196616 | tf_op jit(solution)/shard_map/ppermute | solution.py:100
  55.8 0.9 collective-permute-done.1
  56.6 0.2 fusion.9
  56.9 0.0 copy-done.2
  56.9 0.0 copy-done.3
  56.9 0.7 convolution_bitcast_fusion.1
  57.6 0.7 convolution_bitcast_fusion.4
  58.3 0.7 convolution_bitcast_fusion.2
  59.0 0.7 convolution_bitcast_fusion.3
  59.7 12.5 %all_to_all.32 = f32[4,128,256]{2,1,0:T(8,128)S(1)} all-to-all(f32[4,128,256]{2,1,0:T(8,128)S(1)} %bitcast.78), channel_id=1, replica_groups=mesh['z'=8,'y'=8,'core'=2,'term'=4] {'term'}, dimensions={0} | all-to-all | bytes 1048576 | tf_op jit(solution)/shard_map/all_to_all | solution.py:92
  72.2 0.0 copy-start.1
  72.2 0.4 convolution_multiply_fusion
  72.6 3.7 %collective-permute-start.2 = (f32[256,128]{1,0:T(8,128)S(1)}, f32[256,128]{1,0:T(8,128)S(1)}, u32[]{:S(2)}, u32[]{:S(2)}) collective-permute-start(f32[256,128]{1,0:T(8,128)S(1)} %slice_select_fusion), channel_id=1, source_target_pairs={{0,4},{4,0},{1,5},{5,1},{2,6},{6,2},{3,7},{7,3},{8,12},{12,8},{9,1... | collective-permute-start | bytes 393224 | tf_op jit(solution)/shard_map/ppermute | solution.py:100
  76.4 1.0 collective-permute-done.2
  77.3 12.8 %all_to_all.33 = f32[32,8,128]{2,1,0:T(8,128)S(1)} all-to-all(f32[32,8,128]{2,1,0:T(8,128)S(1)} %add_bitcast_fusion), channel_id=1, replica_groups=mesh['z'=8,'y'=8,'core'=2,'term'=4] {'y','term'}, dimensions={0} | all-to-all | bytes 262144 | tf_op jit(solution)/shard_map/all_to_all | solution.py:92
  90.2 9.2 %all_to_all.34 = f32[8,8,128]{2,1,0:T(8,128)S(1)} all-to-all(f32[8,8,128]{2,1,0:T(8,128)S(1)} %broadcast_in_dim.12), channel_id=1, replica_groups=mesh['z'=8,'y'=8,'core'=2,'term'=4] {'z'}, dimensions={0} | all-to-all | bytes 65536 | tf_op jit(solution)/shard_map/all_to_all | solution.py:92
  99.5 12.6 %all_to_all.35 = f32[32,8,128]{2,1,0:T(8,128)S(1)} all-to-all(f32[32,8,128]{2,1,0:T(8,128)S(1)} %broadcast_in_dim.13), channel_id=1, replica_groups=mesh['z'=8,'y'=8,'core'=2,'term'=4] {'y','term'}, dimensions={0} | all-to-all | bytes 262144 | tf_op jit(solution)/shard_map/all_to_all | solution.py:92
  112.1 6.0 %collective-permute-start.3 = (f32[256,128]{1,0:T(8,128)S(1)}, f32[256,128]{1,0:T(8,128)S(1)}, u32[]{:S(2)}, u32[]{:S(2)}) collective-permute-start(f32[256,128]{1,0:T(8,128)S(1)} %bitcast.79), channel_id=1, source_target_pairs={{0,4},{4,0},{1,5},{5,1},{2,6},{6,2},{3,7},{7,3},{8,12},{12,8},{9,1... | collective-permute-start | bytes 393224 | tf_op jit(solution)/shard_map/ppermute | solution.py:100
  118.1 0.8 collective-permute-done.3
  118.9 0.0 copy-done.1
  118.9 40.0 %shard_map.76 = (f32[256,256]{1,0:T(8,128)S(1)}, f32[256,1]{1,0:T(8,128)S(1)}) custom-call(f32[256,256]{1,0:T(8,128)S(1)} %pad_maximum_fusion.1.window_ref, f32[1,256]{1,0:T(1,128)S(1)} %bitcast.73), custom_call_target="tpu_custom_call" | custom-call | tf_op jit(solution)/shard_map/pallas_call | solution.py:177
  159.0 1.1 fusion.47
  160.0 0.5 fusion
  160.5 1.3 copy.10
  161.8 0.7 reduce
  (17 shorter events, 0.3 us)
Async XLA Ops:
  0.6 0.7 copy-start
  0.6 56.3 %copy-start.2 = (bf16[1,2048,512]{2,1,0:T(8,128)(2,1)S(1)}, bf16[1,2048,512]{2,1,0:T(8,128)(2,1)}, u32[]{:S(2)}) copy-start(bf16[1,2048,512]{2,1,0:T(8,128)(2,1)} %param.5) | copy-start | bytes 6291460
  0.7 3.3 %copy-start.4 = (s32[1,16]{1,0:T(1,128)S(1)}, s32[1,16]{1,0:T(1,128)}, u32[]{:S(2)}) copy-start(s32[1,16]{1,0:T(1,128)} %param.7) | copy-start | bytes 196
  0.7 56.2 %copy-start.3 = (bf16[1,2048,256]{2,1,0:T(8,128)(2,1)S(1)}, bf16[1,2048,256]{2,1,0:T(8,128)(2,1)}, u32[]{:S(2)}) copy-start(bf16[1,2048,256]{2,1,0:T(8,128)(2,1)} %param.8) | copy-start | bytes 3145732
  4.4 9.7 %collective-permute-start = (f32[128,128]{1,0:T(8,128)S(1)}, f32[128,128]{1,0:T(8,128)S(1)}, u32[]{:S(2)}, u32[]{:S(2)}) collective-permute-start(f32[128,128]{1,0:T(8,128)S(1)} %slice_select_fusion.1), channel_id=1, source_target_pairs={{0,4},{4,0},{1,5},{5,1},{2,6},{6,2},{3,7},{7,3},{8,12},{12,8},{9,1... | collective-permute-start | bytes 196616 | tf_op jit(solution)/shard_map/ppermute | solution.py:100
  50.9 5.7 %collective-permute-start.1 = (f32[128,128]{1,0:T(8,128)S(1)}, f32[128,128]{1,0:T(8,128)S(1)}, u32[]{:S(2)}, u32[]{:S(2)}) collective-permute-start(f32[128,128]{1,0:T(8,128)S(1)} %bitcast.80), channel_id=1, source_target_pairs={{0,4},{4,0},{1,5},{5,1},{2,6},{6,2},{3,7},{7,3},{8,12},{12,8},{9,1... | collective-permute-start | bytes 196616 | tf_op jit(solution)/shard_map/ppermute | solution.py:100
  72.2 46.8 %copy-start.1 = (f32[256]{0:T(256)S(1)}, f32[256]{0:T(256)}, u32[]{:S(2)}) copy-start(f32[256]{0:T(256)} %param.9) | copy-start | bytes 3076
  72.6 4.7 %collective-permute-start.2 = (f32[256,128]{1,0:T(8,128)S(1)}, f32[256,128]{1,0:T(8,128)S(1)}, u32[]{:S(2)}, u32[]{:S(2)}) collective-permute-start(f32[256,128]{1,0:T(8,128)S(1)} %slice_select_fusion), channel_id=1, source_target_pairs={{0,4},{4,0},{1,5},{5,1},{2,6},{6,2},{3,7},{7,3},{8,12},{12,8},{9,1... | collective-permute-start | bytes 393224 | tf_op jit(solution)/shard_map/ppermute | solution.py:100
  112.1 6.8 %collective-permute-start.3 = (f32[256,128]{1,0:T(8,128)S(1)}, f32[256,128]{1,0:T(8,128)S(1)}, u32[]{:S(2)}, u32[]{:S(2)}) collective-permute-start(f32[256,128]{1,0:T(8,128)S(1)} %bitcast.79), channel_id=1, source_target_pairs={{0,4},{4,0},{1,5},{5,1},{2,6},{6,2},{3,7},{7,3},{8,12},{12,8},{9,1... | collective-permute-start | bytes 393224 | tf_op jit(solution)/shard_map/ppermute | solution.py:100
where the time goes:
time: 163 us; the launch traced here: 162 us
  blocking collectives  83.8 us (51%)
  Pallas kernels  40 us (25%)
  starting transfers between devices  23.3 us (14%)
  matrix products  7.82 us (5%)
  waiting for transfers between devices  3.49 us (2%)
  local copies, waits for them, and re-layouts  2.08 us (1%)
    all_to_all x6, blocking collectives, all_to_all(): return lax.all_to_all(pieces, axes, 0, 0, tiled=True)  83.8 us
    pallas_call x1, Pallas kernels, shards(): pl.pallas_call(iterate, out_shape=(jax.ShapeDtypeStruct((rank_size, rank_...  40 us
    ppermute x4, starting transfers between devices, swap_cores(): return lax.ppermute(array, 'core', [(0, 1), (1, 0)])  23.3 us
    ppermute x4, waiting for transfers between devices, swap_cores(): return lax.ppermute(array, 'core', [(0, 1), (1, 0)])  3.49 us
  transfers between devices with their start and end apart: 4, of which 4 were waited for; matrix products, arithmetic and copies ran while one was open for 0% of the time, Pallas kernels for 0%

commit v1 on v0

--- a/solution.py
+++ b/solution.py
@@ -1,4 +1,3 @@
-import functools
 import math
 
 import jax
@@ -11,7 +10,6 @@
 
 TERMS = 131072
 ITERS = 4
-SHARE_BLOCKS = 256
 LANES = 128
 PANEL = 16
 OUTER = 128
@@ -66,26 +64,70 @@
             work[end:, :] = work[end:, :] - contract(work[outer:end, end:size], work[outer:end, :], 0, 0)
 
 
-def iterate(window_ref, sv_ref, rotation_ref, singular_ref, gram, work):
+def normalise(work):
+    size = work.shape[0]
+    image = work[:, size:]
+    work[:, :size] = contract(image, image, 1, 1)
+    orthonormal_rows(work)
+
+
+def rotate(
+    window_ref, sv_ref, share_ref, prior_hbm,
+    coords_ref, rows_hbm, singular_ref,
+    gram, work, rotation, prior, rows, load, store,
+):
+    loading = pltpu.make_async_copy(prior_hbm, prior, load)
+    loading.start()
     size = window_ref.shape[0]
     row = lax.broadcasted_iota(jnp.int32, (size, size), 0)
     column = lax.broadcasted_iota(jnp.int32, (size, size), 1)
     sv = sv_ref[...]
-    gram[...] = window_ref[...] + jnp.where(row == column, forget_factor * sv * sv, 0.0)
-    work[:, size:] = gram[...]
-
-    def step(iteration, carry):
-        image = work[:, size:]
-        work[:, :size] = contract(image, image, 1, 1)
-        orthonormal_rows(work)
-        rotation_ref[...] = work[:, size:]
-        work[:, size:] = contract(rotation_ref[...], gram[...], 1, 0)
-        return carry
-
-    lax.fori_loop(0, ITERS, step, 0)
-    singular_ref[...] = jnp.sqrt(
-        jnp.sum(rotation_ref[...] * work[:, size:], axis=1, keepdims=True)
-    )
+    whole = window_ref[...] + jnp.where(row == column, forget_factor * sv * sv, 0.0)
+    gram[...] = whole
+    diagonal = jnp.where(row == column, whole, 0.0)
+    top = jnp.max(jnp.max(diagonal, axis=0, keepdims=True), axis=1, keepdims=True)
+    scaled = whole * (1.0 / top)
+    square = contract(scaled, scaled, 1, 0)
+    work[:, size:] = contract(square, square, 1, 0)
+    normalise(work)
+    result = work[:, size:]
+    miss = contract(result, result, 1, 1) - jnp.where(row == column, 1.0, 0.0)
+    half = jnp.where(row > column, miss, jnp.where(row == column, 0.5 * miss, 0.0))
+    rotation[...] = result - contract(half, result, 1, 0)
+    sound = jnp.sum(miss * miss) < 1e-2
+
+    @pl.when(jnp.logical_not(sound))
+    def _():
+        work[:, size:] = gram[...]
+
+        def step(iteration, carry):
+            normalise(work)
+            rotation[...] = work[:, size:]
+            work[:, size:] = contract(rotation[...], gram[...], 1, 0)
+            return carry
+
+        lax.fori_loop(0, ITERS, step, 0)
+
+    turned = rotation[...]
+    turned_half = turned.astype(jnp.bfloat16)
+    loading.wait()
+    parts = store.shape[0]
+    height = rows.shape[0] // parts
+    storing = []
+    for part in range(parts):
+        span = pl.ds(part * height, height)
+        rows[span, :] = lax.dot_general(
+            prior[span, :], turned_half, (((1,), (1,)), ((), ())), preferred_element_type=jnp.float32
+        ).astype(jnp.bfloat16)
+        copy = pltpu.make_async_copy(rows.at[span], rows_hbm.at[span], store.at[part])
+        copy.start()
+        storing.append(copy)
+    coords_ref[...] = contract(share_ref[...], turned, 1, 1)
+    energy = turned * contract(turned, gram[...], 1, 0)
+    total = contract(jnp.ones((8, size), jnp.float32), energy, 1, 1)
+    singular_ref[...] = jnp.sqrt(total[:1])
+    for copy in storing:
+        copy.wait()
 
 
 def all_to_all(pieces, axes):
@@ -100,17 +142,33 @@
     return lax.ppermute(array, "core", [(0, 1), (1, 0)])
 
 
-def split_cores(array):
-    half = array.shape[0] // 2
-    first = lax.axis_index("core") == 0
-    low, high = array[:half], array[half:]
-    return jnp.where(first, low, high) + swap_cores(jnp.where(first, high, low))
-
-
-def join_cores(half):
-    other = swap_cores(half)
-    first = lax.axis_index("core") == 0
-    return jnp.concatenate([jnp.where(first, half, other), jnp.where(first, other, half)], axis=0)
+def finish(window, prior_sv, share_rows, basis_rows):
+    height, rank_size = basis_rows.shape
+    parts = 4
+    return pl.pallas_call(
+        rotate,
+        in_specs=[pl.BlockSpec(memory_space=pltpu.VMEM)] * 3 + [pl.BlockSpec(memory_space=pl.ANY)],
+        out_specs=(
+            pl.BlockSpec(memory_space=pltpu.VMEM),
+            pl.BlockSpec(memory_space=pl.ANY),
+            pl.BlockSpec(memory_space=pltpu.VMEM),
+        ),
+        out_shape=(
+            jax.ShapeDtypeStruct(share_rows.shape, jnp.float32),
+            jax.ShapeDtypeStruct((height, rank_size), jnp.bfloat16),
+            jax.ShapeDtypeStruct((1, rank_size), jnp.float32),
+        ),
+        scratch_shapes=[
+            pltpu.VMEM((rank_size, rank_size), jnp.float32),
+            pltpu.VMEM((rank_size, 2 * rank_size), jnp.float32),
+            pltpu.VMEM((rank_size, rank_size), jnp.float32),
+            pltpu.VMEM((height, rank_size), jnp.bfloat16),
+            pltpu.VMEM((height, rank_size), jnp.bfloat16),
+            pltpu.SemaphoreType.DMA,
+            pltpu.SemaphoreType.DMA((parts,)),
+        ],
+        compiler_params=pltpu.CompilerParams(vmem_limit_bytes=32 * 2**20),
+    )(window, prior_sv.reshape(1, rank_size), share_rows, basis_rows)
 
 
 def shards(tf_blocks, block_scale, term_blocks, prior_rows, prior_sv):
@@ -136,17 +194,37 @@
     block_sums = jnp.dot(counts, marker, preferred_element_type=jnp.float32)
     scale_rows = jnp.repeat(scales, block_width, axis=0)
     row_mass = jnp.sum(block_sums * scale_rows, axis=1).reshape(stored_blocks, block_width)
-    places = (
-        block_ids[:, None] == jnp.arange(SHARE_BLOCKS, dtype=jnp.int32)[None, :]
-    ).astype(jnp.float32)
-    dense = jnp.dot(places.T, row_mass, precision=highest)
-    chips = ("z", "y")
-    chip_count = planes * lines
-    half_mass = split_cores(dense).reshape(chip_count, -1, block_width)
-    own_mass = jnp.sum(all_to_all(half_mass, chips), axis=0)
-    half_mass = all_to_all(repeat(own_mass, chip_count), chips).reshape(-1, block_width)
-    share_mass = join_cores(half_mass)
-    term_mass = jnp.dot(places, share_mass, precision=highest)
+    half_width = block_width // 2
+    id_values = block_ids.astype(jnp.float32)
+    tail = jnp.pad(id_values, (0, LANES - stored_blocks))
+    halves = jnp.stack(
+        [
+            jnp.concatenate([row_mass[:, side : side + half_width].reshape(-1), tail])
+            for side in (0, half_width)
+        ]
+    )
+    outgoing = jnp.broadcast_to(halves[None], (doc_count // 2,) + halves.shape)
+    incoming = all_to_all(outgoing.reshape(doc_count, 1, -1), ("z", "y", "core"))
+    incoming = incoming.reshape(doc_count, -1, LANES)
+    slots = LANES // half_width
+    slot_rows = stored_blocks // slots
+    masses = incoming[:, :slot_rows].reshape(doc_count * slot_rows, LANES)
+    all_ids = incoming[:, slot_rows, :stored_blocks]
+    chip = lax.axis_index("z") * lines + lax.axis_index("y")
+    pair_ids = lax.dynamic_slice_in_dim(all_ids, 2 * chip, 2, 0).reshape(-1)
+    pair_mass = 0.0
+    for slot in range(slots):
+        slot_ids = all_ids[:, slot::slots].reshape(-1)
+        matches = (pair_ids[:, None] == slot_ids[None, :]).astype(jnp.float32)
+        found = jnp.dot(matches, masses, precision=highest)
+        pair_mass = pair_mass + found[:, slot * half_width : (slot + 1) * half_width]
+    first = lax.axis_index("core") == 0
+    low, high = pair_mass[:stored_blocks], pair_mass[stored_blocks:]
+    mine = jnp.where(first, low, high)
+    other = swap_cores(jnp.where(first, high, low))
+    term_mass = jnp.concatenate(
+        [jnp.where(first, mine, other), jnp.where(first, other, mine)], axis=1
+    )
     weight = jnp.log(1.0 + total_docs / (1.0 + term_mass)).reshape(height)
     root_terms = math.sqrt(TERMS)
     pieces = []
@@ -165,32 +243,15 @@
     own_gram = jnp.dot(share_rows.T, share_rows, precision=highest) / total_docs
     flat_gram = jnp.concatenate([own_gram[:, t : t + LANES] for t in range(0, rank_size, LANES)])
     plane = ("y", "term")
+    across = ("z", "core")
     plane_count = lines * term_count
-    half_gram = split_cores(flat_gram).reshape(plane_count, -1, LANES)
-    plane_gram = jnp.sum(all_to_all(half_gram, plane), axis=0)
-    piece_gram = jnp.sum(all_to_all(repeat(plane_gram, planes), "z"), axis=0)
-    half_gram = all_to_all(repeat(piece_gram, plane_count), plane).reshape(-1, LANES)
-    flat_gram = join_cores(half_gram)
+    plane_gram = jnp.sum(all_to_all(flat_gram.reshape(plane_count, -1, LANES), plane), axis=0)
+    piece_gram = jnp.sum(all_to_all(repeat(plane_gram, doc_count // lines), across), axis=0)
+    flat_gram = all_to_all(repeat(piece_gram, plane_count), plane).reshape(-1, LANES)
     window = jnp.concatenate(
         [flat_gram[t : t + rank_size] for t in range(0, flat_gram.shape[0], rank_size)], axis=1
     )
-    rotation, singular = pl.pallas_call(
-        iterate,
-        out_shape=(
-            jax.ShapeDtypeStruct((rank_size, rank_size), jnp.float32),
-            jax.ShapeDtypeStruct((rank_size, 1), jnp.float32),
-        ),
-        scratch_shapes=[
-            pltpu.VMEM((rank_size, rank_size), jnp.float32),
-            pltpu.VMEM((rank_size, 2 * rank_size), jnp.float32),
-        ],
-        compiler_params=pltpu.CompilerParams(vmem_limit_bytes=32 * 2**20),
-    )(window, prior_sv.reshape(1, rank_size))
-    doc_coords = contract(share_rows, rotation, 1, 1)
-    rotation_half = rotation.astype(jnp.bfloat16)
-    new_rows = lax.dot_general(
-        basis_rows, rotation_half, (((1,), (1,)), ((), ())), preferred_element_type=jnp.float32
-    ).astype(jnp.bfloat16)
+    doc_coords, new_rows, singular = finish(window, prior_sv, share_rows, basis_rows)
     return (doc_coords, new_rows[None], singular.reshape(rank_size))
 
 

time: 163 us -> 169 us (1.037)
  blocking collectives: 83.8 us -> 57.7 us
  waiting for transfers between devices: 3.49 us -> 23.1 us
  Pallas kernels: 40 us -> 54.2 us
  starting transfers between devices: 23.3 us -> 20.3 us
  local copies, waits for them, and re-layouts: 2.08 us -> 3.83 us
    all_to_all x6 -> x4, blocking collectives: 83.8 us -> 57.7 us  [all_to_all(): return lax.all_to_all(pieces, axes, 0, 0, tiled=True)]
    all_to_all x0 -> x1, waiting for transfers between devices: none -> 22 us  [all_to_all(): return lax.all_to_all(pieces, axes, 0, 0, tiled=True)]
    ppermute x4 -> x1, starting transfers between devices: 23.3 us -> 1.92 us  [swap_cores(): return lax.ppermute(array, 'core', [(0, 1), (1, 0)])]
    all_to_all x0 -> x1, starting transfers between devices: none -> 18.4 us  [all_to_all(): return lax.all_to_all(pieces, axes, 0, 0, tiled=True)]
    pallas_call x1, Pallas kernels: 40 us -> 54.2 us  [finish(): pl.pallas_call(rotate, in_specs=[pl.BlockSpec(memory_space=pltpu.VMEM)] *...]
    ppermute x4 -> x1, waiting for transfers between devices: 3.49 us -> 1.12 us  [swap_cores(): return lax.ppermute(array, 'core', [(0, 1), (1, 0)])]
    unnamed x13 -> x10, local copies, waits for them, and re-layouts: 2.04 us -> 0.11 us
    reshape x0 -> x3, local copies, waits for them, and re-layouts: none -> 1.83 us  [the longest x1 1.69 us: shards(): outgoing.reshape(doc_count, 1, -1)]
  transfers between devices with their start and end apart: 4 -> 2, of which waited for: 4 -> 2; matrix products, arithmetic and copies ran while one was open for 0% -> 0% of each run, Pallas kernels for 0% -> 0%
where the time goes in v1:
time: 169 us; the launch traced here: 168 us
  blocking collectives  57.7 us (34%)
  Pallas kernels  54.2 us (32%)
  waiting for transfers between devices  23.1 us (14%)
  starting transfers between devices  20.3 us (12%)
  matrix products  7.28 us (4%)
  local copies, waits for them, and re-layouts  3.83 us (2%)
    all_to_all x4, blocking collectives, all_to_all(): return lax.all_to_all(pieces, axes, 0, 0, tiled=True)  57.7 us
    pallas_call x1, Pallas kernels, finish(): pl.pallas_call(rotate, in_specs=[pl.BlockSpec(memory_space=pltpu.VMEM)] *...  54.2 us
    all_to_all x1, waiting for transfers between devices, all_to_all(): return lax.all_to_all(pieces, axes, 0, 0, tiled=True)  22 us
    all_to_all x1, starting transfers between devices, all_to_all(): return lax.all_to_all(pieces, axes, 0, 0, tiled=True)  18.4 us
    dot_general x4, matrix products, shards(): lax.dot_general(doc_block, basis_half, (((0,), (0,)), ((), ())), preferre...  3.77 us
  transfers between devices with their start and end apart: 2, of which 2 were waited for; matrix products, arithmetic and copies ran while one was open for 0% of the time, Pallas kernels for 0%

profile of v1, /device:TPU:1, one launch (start us, length us, event | category | flops | bytes accessed | tf_op | source)
XLA Modules:
  0.0 168.5 jit_solution(14802121559616098007)
XLA Ops:
  0.6 0.0 copy-start
  0.7 0.7 convert_bitcast_fusion
  1.3 0.0 copy-done
  1.3 0.1 broadcast_bitcast_fusion
  1.4 2.4 %fusion.5 = f32[2048]{0:T(1024)S(1)} fusion(s32[512]{0:T(512)S(1)} %add_select_fusion, bf16[1,2048,512]{2,1,0:T(8,128)(2,1)} %param.5, f32[1,4,16,128]{3,2,1,0:T(8,128)S(1)} %broadcast_bitcast_fusion), kind=kOutput, calls=%fused_computation.15 | convolution fusion | flops 8407040 | bytes 2140160 | tf_op jit(solution)/shard_map/dot_general | solution.py:194
  3.8 0.1 fusion.50
  3.9 0.1 reshape.121
  3.9 0.1 reshape.122
  4.0 0.2 broadcast_in_dim.11
  4.2 1.7 %reshape.130 = f32[128,1,1152]{2,1,0:T(1,128)} reshape(f32[64,2,1152]{2,1,0:T(2,128)S(1)} %broadcast_in_dim.11) | data formatting | bytes 1179648 | tf_op jit(solution)/shard_map/reshape | solution.py:207
  5.9 18.4 %all-to-all-start = ((f32[128,1,1152]{2,1,0:T(1,128)}), f32[128,1,1152]{2,1,0:T(1,128)S(1)}, u32[]{:S(2)}, u32[]{:S(2)}) async-start(f32[128,1,1152]{2,1,0:T(1,128)} %reshape.130), calls=%async_computation | async-start | bytes 1179648 | tf_op jit(solution)/shard_map/all_to_all | solution.py:134
  24.3 22.0 %all-to-all-done = f32[128,1,1152]{2,1,0:T(1,128)S(1)} async-done(((f32[128,1,1152]{2,1,0:T(1,128)}), f32[128,1,1152]{2,1,0:T(1,128)S(1)}, u32[]{:S(2)}, u32[]{:S(2)}) %all-to-all-start) | async-done | bytes 589856 | tf_op jit(solution)/shard_map/all_to_all | solution.py:134
  46.3 0.7 copy.24
  46.9 0.0 copy-start.1
  47.0 0.1 constant_dynamic-slice_fusion
  47.1 0.1 copy.25
  47.2 0.1 eq.50
  47.3 0.2 copy.27
  47.5 0.1 copy.26
  47.6 0.1 eq.52
  47.7 0.1 copy.28
  47.8 0.1 eq.55
  47.9 0.0 copy-start.3
  47.9 0.3 fusion.19
  48.3 0.4 convolution_add_fusion
  48.7 1.9 %collective-permute-start = (f32[16,64]{1,0:T(8,128)S(1)}, f32[16,64]{1,0:T(8,128)S(1)}, u32[]{:S(2)}, u32[]{:S(2)}) collective-permute-start(f32[16,64]{1,0:T(8,128)S(1)} %slice_select_fusion), channel_id=1, source_target_pairs={{0,4},{4,0},{1,5},{5,1},{2,6},{6,2},{3,7},{7,3},{8,12},{12,8},{9,1... | collective-permute-start | bytes 12296 | tf_op jit(solution)/shard_map/ppermute | solution.py:142
  50.6 1.1 collective-permute-done
  51.7 0.1 fusion.38
  51.9 0.0 copy-done.1
  51.9 1.7 %convolution_bitcast_fusion.1 = f32[128,256]{1,0:T(8,128)S(1)} fusion(f32[2048]{0:T(1024)S(1)} %bitcast.88, bf16[2048,512]{1,0:T(8,128)(2,1)} %bitcast.74, bf16[1,2048,256]{2,1,0:T(8,128)(2,1)S(1)} %copy-done.1), kind=kOutput, calls=%fused_computation.11 | convolution fusion | flops 135790592 | bytes 1712128 | tf_op jit(solution)/shard_map/dot_general | solution.py:237
  53.6 0.0 copy-done.3
  53.6 0.7 convolution_bitcast_fusion.4
  54.3 0.7 convolution_bitcast_fusion.2
  55.0 0.7 convolution_bitcast_fusion.3
  55.8 13.0 %all_to_all.25 = f32[4,128,256]{2,1,0:T(8,128)S(1)} all-to-all(f32[4,128,256]{2,1,0:T(8,128)S(1)} %bitcast.78), channel_id=1, replica_groups=mesh['z'=8,'y'=8,'core'=2,'term'=4] {'term'}, dimensions={0} | all-to-all | bytes 1048576 | tf_op jit(solution)/shard_map/all_to_all | solution.py:134
  68.8 0.4 convolution_multiply_fusion
  69.2 0.0 copy-start.2
  69.2 14.0 %all_to_all.26 = f32[32,16,128]{2,1,0:T(8,128)S(1)} all-to-all(f32[32,16,128]{2,1,0:T(8,128)S(1)} %bitcast.79), channel_id=1, replica_groups=mesh['z'=8,'y'=8,'core'=2,'term'=4] {'y','term'}, dimensions={0} | all-to-all | bytes 524288 | tf_op jit(solution)/shard_map/all_to_all | solution.py:134
  83.3 15.4 %all_to_all.27 = f32[16,16,128]{2,1,0:T(8,128)S(1)} all-to-all(f32[16,16,128]{2,1,0:T(8,128)S(1)} %broadcast_in_dim.12), channel_id=1, replica_groups=mesh['z'=8,'y'=8,'core'=2,'term'=4] {'z','core'}, dimensions={0} | all-to-all | bytes 262144 | tf_op jit(solution)/shard_map/all_to_all | solution.py:134
  98.7 15.4 %all_to_all.28 = f32[32,16,128]{2,1,0:T(8,128)S(1)} all-to-all(f32[32,16,128]{2,1,0:T(8,128)S(1)} %broadcast_in_dim.13), channel_id=1, replica_groups=mesh['z'=8,'y'=8,'core'=2,'term'=4] {'y','term'}, dimensions={0} | all-to-all | bytes 524288 | tf_op jit(solution)/shard_map/all_to_all | solution.py:134
  114.1 0.0 copy-done.2
  114.1 54.2 %shard_map.76 = (f32[128,256]{1,0:T(8,128)}, bf16[2048,256]{1,0:T(8,128)(2,1)}, f32[1,256]{1,0:T(1,128)}) custom-call(f32[256,256]{1,0:T(8,128)S(1)} %pad_maximum_fusion.2.window_ref, f32[1,256]{1,0:T(1,128)S(1)} %bitcast.69, f32[128,256]{1,0:T(8,128)S(1)} %reduce_sum.37.share_ref, bf16[2048,256]{1,0:T(8,128)(2,1)S(1)} %bitcast.68), custom_call_target="tpu_custom_call" | custom-call | tf_op jit(solution)/shard_map/pallas_call | solution.py:148
  (23 shorter events, 0.4 us)
Async XLA Ops:
  0.6 0.7 copy-start
  5.9 40.4 %all-to-all-start = ((f32[128,1,1152]{2,1,0:T(1,128)}), f32[128,1,1152]{2,1,0:T(1,128)S(1)}, u32[]{:S(2)}, u32[]{:S(2)}) async-start(f32[128,1,1152]{2,1,0:T(1,128)} %reshape.130), calls=%async_computation | async-start | bytes 1179648 | tf_op jit(solution)/shard_map/all_to_all | solution.py:134
  46.9 4.9 %copy-start.1 = (bf16[1,2048,256]{2,1,0:T(8,128)(2,1)S(1)}, bf16[1,2048,256]{2,1,0:T(8,128)(2,1)}, u32[]{:S(2)}) copy-start(bf16[1,2048,256]{2,1,0:T(8,128)(2,1)} %param.8) | copy-start | bytes 3145732
  47.9 5.7 %copy-start.3 = (bf16[1,2048,512]{2,1,0:T(8,128)(2,1)S(1)}, bf16[1,2048,512]{2,1,0:T(8,128)(2,1)}, u32[]{:S(2)}) copy-start(bf16[1,2048,512]{2,1,0:T(8,128)(2,1)} %param.5) | copy-start | bytes 6291460
  48.7 3.1 %collective-permute-start = (f32[16,64]{1,0:T(8,128)S(1)}, f32[16,64]{1,0:T(8,128)S(1)}, u32[]{:S(2)}, u32[]{:S(2)}) collective-permute-start(f32[16,64]{1,0:T(8,128)S(1)} %slice_select_fusion), channel_id=1, source_target_pairs={{0,4},{4,0},{1,5},{5,1},{2,6},{6,2},{3,7},{7,3},{8,12},{12,8},{9,1... | collective-permute-start | bytes 12296 | tf_op jit(solution)/shard_map/ppermute | solution.py:142
  69.2 45.0 %copy-start.2 = (f32[256]{0:T(256)S(1)}, f32[256]{0:T(256)}, u32[]{:S(2)}) copy-start(f32[256]{0:T(256)} %param.9) | copy-start | bytes 3076

commit v2 on v1

--- a/solution.py
+++ b/solution.py
@@ -1,3 +1,4 @@
+import functools
 import math
 
 import jax
@@ -171,74 +172,180 @@
     )(window, prior_sv.reshape(1, rank_size), share_rows, basis_rows)
 
 
+def mass_pieces_kernel(slots, counts_ref, scale_ref, ids_ref, pieces_ref, mass):
+    step = pl.program_id(0)
+    width = counts_ref.shape[0] // slots
+    docs = counts_ref.shape[1]
+    doc_blocks = scale_ref.shape[0]
+    marker = (
+        lax.broadcasted_iota(jnp.int32, (16, docs), 1) // (docs // doc_blocks)
+        == lax.broadcasted_iota(jnp.int32, (16, docs), 0)
+    ).astype(jnp.bfloat16)
+    for slot in range(slots):
+        block = counts_ref[slot * width : (slot + 1) * width, :]
+        sums = lax.dot_general(
+            marker, block, (((1,), (1,)), ((), ())), preferred_element_type=jnp.float32
+        )
+        place = step * slots + slot
+        total = sums[0:1] * scale_ref[0, place]
+        for j in range(1, doc_blocks):
+            total = total + sums[j : j + 1] * scale_ref[j, place]
+        mass[pl.ds(place, 1), :] = total
+
+    @pl.when(step == pl.num_programs(0) - 1)
+    def _():
+        stored = mass.shape[0]
+        even = jnp.concatenate([mass[q : q + 1, :] for q in range(0, stored, 2)], axis=0)
+        odd = jnp.concatenate([mass[q : q + 1, :] for q in range(1, stored, 2)], axis=0)
+        half = LANES // 2
+        lower = lax.broadcasted_iota(jnp.int32, even.shape, 1) < half
+        near = jnp.where(lower, even, pltpu.roll(odd, half, 1))
+        far = jnp.where(lower, pltpu.roll(even, half, 1), odd)
+        ids = jnp.concatenate(
+            [ids_ref[...].astype(jnp.float32), jnp.full((1, LANES - stored), -1.0, jnp.float32)], axis=1
+        )
+        period = jnp.concatenate([near, ids, far, ids] * 4, axis=0)
+        rows = period.shape[0]
+        for part in range(pieces_ref.shape[0] // rows):
+            pieces_ref[part * rows : (part + 1) * rows, :] = period
+
+
+def mass_pieces(counts, scales, block_ids, doc_count):
+    height, docs = counts.shape
+    stored = block_ids.shape[0]
+    steps = 4
+    return pl.pallas_call(
+        functools.partial(mass_pieces_kernel, stored // steps),
+        grid=(steps,),
+        in_specs=[
+            pl.BlockSpec((height // steps, docs), lambda i: (i, 0)),
+            pl.BlockSpec(memory_space=pltpu.SMEM),
+            pl.BlockSpec((1, stored), lambda i: (0, 0)),
+        ],
+        out_specs=pl.BlockSpec((doc_count * (stored // 2 + 1), LANES), lambda i: (0, 0)),
+        out_shape=jax.ShapeDtypeStruct((doc_count * (stored // 2 + 1), LANES), jnp.float32),
+        scratch_shapes=[pltpu.VMEM((stored, height // stored), jnp.float32)],
+        compiler_params=pltpu.CompilerParams(vmem_limit_bytes=56 * 2**20),
+    )(counts, scales.T, block_ids.reshape(1, stored))
+
+
+def find_masses_kernel(stored, place_ref, incoming_ref, keep_ref, send_ref):
+    piece = stored // 2 + 1
+    batches = incoming_ref.shape[0] // piece
+    half = LANES // 2
+    chip, core = place_ref[0], place_ref[1]
+    ids = incoming_ref[pl.ds(piece - 1, batches, stride=piece), :].T[:stored]
+    batch = lax.broadcasted_iota(jnp.int32, ids.shape, 1)
+    pair = [
+        jnp.sum(jnp.where(batch == 2 * chip + side, ids, 0.0), axis=1, keepdims=True)
+        for side in (0, 1)
+    ]
+    wanted = jnp.broadcast_to(jnp.concatenate(pair, axis=0), (2 * stored, batches))
+    matches, parts = [], [[], [], []]
+    for row in range(piece - 1):
+        masses = incoming_ref[pl.ds(row, batches, stride=piece), :]
+        high = masses.astype(jnp.bfloat16)
+        rest = masses - high.astype(jnp.float32)
+        low = rest.astype(jnp.bfloat16)
+        last = (rest - low.astype(jnp.float32)).astype(jnp.bfloat16)
+        for part, value in zip(parts, (high, low, last)):
+            part.append(value)
+        match = [
+            jnp.where(wanted == ids[2 * row + slot : 2 * row + slot + 1], 1.0, 0.0)
+            for slot in range(2)
+        ]
+        matches.append(jnp.concatenate(match, axis=0).astype(jnp.bfloat16))
+    matches = jnp.concatenate(matches, axis=1)
+    found = 0.0
+    for part in parts:
+        found = found + jnp.dot(
+            matches, jnp.concatenate(part, axis=0), preferred_element_type=jnp.float32
+        )
+    masses = found[: 2 * stored, :half] + found[2 * stored :, half:]
+    mine = core == 0
+    keep_ref[...] = jnp.where(mine, masses[:stored], masses[stored:])
+    send_ref[...] = jnp.where(mine, masses[stored:], masses[:stored])
+
+
+def find_masses(incoming, chip, core, stored):
+    shape = jax.ShapeDtypeStruct((stored, LANES // 2), jnp.float32)
+    return pl.pallas_call(
+        functools.partial(find_masses_kernel, stored),
+        in_specs=[
+            pl.BlockSpec(memory_space=pltpu.SMEM),
+            pl.BlockSpec(memory_space=pltpu.VMEM),
+        ],
+        out_specs=(pl.BlockSpec(memory_space=pltpu.VMEM), pl.BlockSpec(memory_space=pltpu.VMEM)),
+        out_shape=(shape, shape),
+        compiler_params=pltpu.CompilerParams(vmem_limit_bytes=16 * 2**20),
+    )(jnp.stack([chip, core]).astype(jnp.int32), incoming)
+
+
+def project_kernel(
+    total_docs, core_ref, keep_ref, come_ref, scale_ref, prior_ref, turned_ref, partial_ref, basis
+):
+    stored = keep_ref.shape[0]
+    doc_blocks = scale_ref.shape[0]
+    height = prior_ref.shape[0]
+    width = height // stored
+    docs = partial_ref.shape[0] // doc_blocks
+    mine, other = keep_ref[...], come_ref[...]
+    first = core_ref[0] == 0
+    term_mass = jnp.concatenate(
+        [jnp.where(first, mine, other), jnp.where(first, other, mine)], axis=1
+    )
+    weight = jnp.log(1.0 + total_docs / (1.0 + term_mass))
+    spare = jnp.zeros((LANES - stored, LANES), jnp.float32)
+    turned_weight = jnp.concatenate([weight, spare], axis=0).T[:, :stored]
+    columns = [turned_weight * scale_ref[j : j + 1, :] / math.sqrt(TERMS) for j in range(doc_blocks)]
+    for block in range(stored):
+        span = slice(block * width, (block + 1) * width)
+        prior = prior_ref[span, :].astype(jnp.float32)
+        for j in range(doc_blocks):
+            basis[j, span, :] = (prior * columns[j][:, block : block + 1]).astype(jnp.bfloat16)
+    for j in range(doc_blocks):
+        partial_ref[j * docs : (j + 1) * docs, :] = jnp.dot(
+            turned_ref[j * docs : (j + 1) * docs, :], basis[j], preferred_element_type=jnp.float32
+        )
+
+
+def project(core, keep, come, scales, prior, turned, total_docs):
+    height, rank_size = prior.shape
+    docs = turned.shape[0]
+    doc_blocks = scales.shape[1]
+    vmem = pl.BlockSpec(memory_space=pltpu.VMEM)
+    return pl.pallas_call(
+        functools.partial(project_kernel, total_docs),
+        in_specs=[pl.BlockSpec(memory_space=pltpu.SMEM)] + [vmem] * 5,
+        out_specs=vmem,
+        out_shape=jax.ShapeDtypeStruct((docs, rank_size), jnp.float32),
+        scratch_shapes=[pltpu.VMEM((doc_blocks, height, rank_size), jnp.bfloat16)],
+        compiler_params=pltpu.CompilerParams(vmem_limit_bytes=32 * 2**20),
+    )(core.reshape(1).astype(jnp.int32), keep, come, scales.T, prior, turned)
+
+
 def shards(tf_blocks, block_scale, term_blocks, prior_rows, prior_sv):
     counts = tf_blocks[0]
     scales = block_scale[0]
     block_ids = term_blocks[0]
     basis_rows = prior_rows[0]
     stored_blocks = block_ids.shape[0]
-    height = counts.shape[0]
-    block_width = height // stored_blocks
     batch_docs = counts.shape[1]
-    doc_blocks = batch_docs // block_width
     rank_size = basis_rows.shape[1]
     planes, lines = lax.axis_size("z"), lax.axis_size("y")
     doc_count = planes * lines * lax.axis_size("core")
     term_count = lax.axis_size("term")
     total_docs = batch_docs * doc_count
     share_docs = batch_docs // term_count
-    marker = (
-        jnp.arange(batch_docs, dtype=jnp.int32)[:, None] // block_width
-        == jnp.arange(doc_blocks, dtype=jnp.int32)[None, :]
-    ).astype(jnp.bfloat16)
-    block_sums = jnp.dot(counts, marker, preferred_element_type=jnp.float32)
-    scale_rows = jnp.repeat(scales, block_width, axis=0)
-    row_mass = jnp.sum(block_sums * scale_rows, axis=1).reshape(stored_blocks, block_width)
-    half_width = block_width // 2
-    id_values = block_ids.astype(jnp.float32)
-    tail = jnp.pad(id_values, (0, LANES - stored_blocks))
-    halves = jnp.stack(
-        [
-            jnp.concatenate([row_mass[:, side : side + half_width].reshape(-1), tail])
-            for side in (0, half_width)
-        ]
-    )
-    outgoing = jnp.broadcast_to(halves[None], (doc_count // 2,) + halves.shape)
-    incoming = all_to_all(outgoing.reshape(doc_count, 1, -1), ("z", "y", "core"))
-    incoming = incoming.reshape(doc_count, -1, LANES)
-    slots = LANES // half_width
-    slot_rows = stored_blocks // slots
-    masses = incoming[:, :slot_rows].reshape(doc_count * slot_rows, LANES)
-    all_ids = incoming[:, slot_rows, :stored_blocks]
+    pieces = mass_pieces(counts, scales, block_ids, doc_count)
+    incoming = all_to_all(pieces.reshape(doc_count, 1, -1), ("z", "y", "core"))
+    turned = counts.T
     chip = lax.axis_index("z") * lines + lax.axis_index("y")
-    pair_ids = lax.dynamic_slice_in_dim(all_ids, 2 * chip, 2, 0).reshape(-1)
-    pair_mass = 0.0
-    for slot in range(slots):
-        slot_ids = all_ids[:, slot::slots].reshape(-1)
-        matches = (pair_ids[:, None] == slot_ids[None, :]).astype(jnp.float32)
-        found = jnp.dot(matches, masses, precision=highest)
-        pair_mass = pair_mass + found[:, slot * half_width : (slot + 1) * half_width]
-    first = lax.axis_index("core") == 0
-    low, high = pair_mass[:stored_blocks], pair_mass[stored_blocks:]
-    mine = jnp.where(first, low, high)
-    other = swap_cores(jnp.where(first, high, low))
-    term_mass = jnp.concatenate(
-        [jnp.where(first, mine, other), jnp.where(first, other, mine)], axis=1
-    )
-    weight = jnp.log(1.0 + total_docs / (1.0 + term_mass)).reshape(height)
-    root_terms = math.sqrt(TERMS)
-    pieces = []
-    for column in range(doc_blocks):
-        basis_half = (
-            basis_rows * (weight * scale_rows[:, column] / root_terms)[:, None]
-        ).astype(jnp.bfloat16)
-        doc_block = counts[:, column * block_width : (column + 1) * block_width]
-        pieces.append(
-            lax.dot_general(
-                doc_block, basis_half, (((0,), (0,)), ((), ())), preferred_element_type=jnp.float32
-            )
-        )
-    partial = jnp.concatenate(pieces, axis=0).reshape(term_count, share_docs, rank_size)
+    core = lax.axis_index("core")
+    keep, send = find_masses(incoming.reshape(-1, LANES), chip, core, stored_blocks)
+    come = swap_cores(send)
+    partial = project(core, keep, come, scales, basis_rows, turned, total_docs)
+    partial = partial.reshape(term_count, share_docs, rank_size)
     share_rows = jnp.sum(all_to_all(partial, "term"), axis=0)
     own_gram = jnp.dot(share_rows.T, share_rows, precision=highest) / total_docs
     flat_gram = jnp.concatenate([own_gram[:, t : t + LANES] for t in range(0, rank_size, LANES)])

time: 169 us -> 167 us (0.988)
  matrix products: 7.28 us -> 0.41 us
  Pallas kernels: 54.2 us -> 60.9 us
    dot_general x7 -> x0, matrix products: 6.87 us -> none  [the longest x4 3.77 us: shards(): lax.dot_general(doc_block, basis_half, (((0,), (0,)), ((), ())), preferre...]
    pallas_call x0 -> x3, Pallas kernels: none -> 6.73 us  [the longest x1 3.86 us: mass_pieces(): pl.pallas_call(functools.partial(mass_pieces_kernel, stored // steps), gr...]
    unnamed x10 -> x7, local copies, waits for them, and re-layouts: 0.11 us -> 2.95 us
    reshape x3 -> x0, local copies, waits for them, and re-layouts: 1.83 us -> none  [the longest x1 1.69 us: shards(): outgoing.reshape(doc_count, 1, -1)]
  transfers between devices with their start and end apart: 2 -> 2, of which waited for: 2 -> 1; matrix products, arithmetic and copies ran while one was open for 0% -> 2% of each run, Pallas kernels for 0% -> 0%
where the time goes in v2:
time: 167 us; the launch traced here: 166 us
  Pallas kernels  60.9 us (36%)
  blocking collectives  58.5 us (35%)
  waiting for transfers between devices  21.9 us (13%)
  starting transfers between devices  20.5 us (12%)
  local copies, waits for them, and re-layouts  3.01 us (2%)
    all_to_all x4, blocking collectives, all_to_all(): return lax.all_to_all(pieces, axes, 0, 0, tiled=True)  58.5 us
    pallas_call x1, Pallas kernels, finish(): pl.pallas_call(rotate, in_specs=[pl.BlockSpec(memory_space=pltpu.VMEM)] *...  54.2 us
    all_to_all x1, waiting for transfers between devices, all_to_all(): return lax.all_to_all(pieces, axes, 0, 0, tiled=True)  21.9 us
    all_to_all x1, starting transfers between devices, all_to_all(): return lax.all_to_all(pieces, axes, 0, 0, tiled=True)  18.4 us
    pallas_call x1, Pallas kernels, mass_pieces(): pl.pallas_call(functools.partial(mass_pieces_kernel, stored // steps), gr...  3.86 us
  transfers between devices with their start and end apart: 2, of which 1 were waited for; matrix products, arithmetic and copies ran while one was open for 2% of the time, Pallas kernels for 0%

profile of v2, /device:TPU:1, one launch (start us, length us, event | category | flops | bytes accessed | tf_op | source)
XLA Modules:
  0.0 166.4 jit_solution(9516798167993283559)
XLA Ops:
  0.6 3.9 %shard_map.76 = f32[1152,128]{1,0:T(8,128)} custom-call(bf16[2048,512]{1,0:T(8,128)(2,1)} %bitcast.29, f32[4,16]{1,0:T(4,128)} %bitcast.26, s32[1,16]{1,0:T(1,128)} %ids_ref.1), custom_call_target="tpu_custom_call" | custom-call | tf_op jit(solution)/shard_map/pallas_call | solution.py:217
  4.5 18.4 %all-to-all-start = ((f32[128,1,1152]{2,1,0:T(1,128)}), f32[128,1,1152]{2,1,0:T(1,128)S(1)}, u32[]{:S(2)}, u32[]{:S(2)}) async-start(f32[128,1,1152]{2,1,0:T(1,128)} %bitcast.30), calls=%async_computation | async-start | bytes 1179648 | tf_op jit(solution)/shard_map/all_to_all | solution.py:135
  22.9 0.1 pad_add_fusion.place_ref
  23.0 21.9 %all-to-all-done = f32[128,1,1152]{2,1,0:T(1,128)S(1)} async-done(((f32[128,1,1152]{2,1,0:T(1,128)}), f32[128,1,1152]{2,1,0:T(1,128)S(1)}, u32[]{:S(2)}, u32[]{:S(2)}) %all-to-all-start) | async-done | bytes 589856 | tf_op jit(solution)/shard_map/all_to_all | solution.py:135
  44.9 1.1 shard_map.77
  45.9 0.0 copy-start
  46.0 0.0 copy-start.1
  46.0 2.1 %collective-permute-start = (f32[16,64]{1,0:T(8,128)S(1)}, f32[16,64]{1,0:T(8,128)S(1)}, u32[]{:S(2)}, u32[]{:S(2)}) collective-permute-start(f32[16,64]{1,0:T(8,128)S(1)} %get-tuple-element.9), channel_id=1, source_target_pairs={{0,4},{4,0},{1,5},{5,1},{2,6},{6,2},{3,7},{7,3},{8,12},{12,8},{9,1... | collective-permute-start | bytes 12296 | tf_op jit(solution)/shard_map/ppermute | solution.py:143
  48.0 2.9 %copy.13 = bf16[1,2048,512]{1,2,0:T(8,128)(2,1)S(1)} copy(bf16[1,2048,512]{2,1,0:T(8,128)(2,1)} %param.5) | data formatting | bytes 4194304 | tf_op args[0]
  51.0 0.0 collective-permute-done.come_ref
  51.0 0.0 copy-done
  51.0 0.0 copy-done.1
  51.0 1.8 %shard_map.78 = f32[512,256]{1,0:T(8,128)S(1)} custom-call(s32[1]{0:T(128)} %bitcast.core_ref, f32[16,64]{1,0:T(8,128)S(1)} %get-tuple-element.8.keep_ref, f32[16,64]{1,0:T(8,128)S(1)} %collective-permute-done.come_ref, f32[4,16]{1,0:T(4,128)S(1)} %bitcast.27, bf16[2048,256]{1,0:T(8,128)(2,1)S(1)} %bitcast.22, bf16[512,2048]{1,0:T(8,128)(2,1)S(1)} %bitcast.21), custom_call_target="tpu_custom_call" | custom-call | tf_op jit(solution)/shard_map/pallas_call | solution.py:317
  52.8 12.3 %all_to_all.25 = f32[4,128,256]{2,1,0:T(8,128)S(1)} all-to-all(f32[4,128,256]{2,1,0:T(8,128)S(1)} %bitcast.25), channel_id=1, replica_groups=mesh['z'=8,'y'=8,'core'=2,'term'=4] {'term'}, dimensions={0} | all-to-all | bytes 1048576 | tf_op jit(solution)/shard_map/all_to_all | solution.py:135
  65.1 0.4 convolution_multiply_fusion
  65.6 0.0 copy-start.2
  65.6 15.5 %all_to_all.26 = f32[32,16,128]{2,1,0:T(8,128)S(1)} all-to-all(f32[32,16,128]{2,1,0:T(8,128)S(1)} %bitcast.31), channel_id=1, replica_groups=mesh['z'=8,'y'=8,'core'=2,'term'=4] {'y','term'}, dimensions={0} | all-to-all | bytes 524288 | tf_op jit(solution)/shard_map/all_to_all | solution.py:135
  81.2 15.1 %all_to_all.27 = f32[16,16,128]{2,1,0:T(8,128)S(1)} all-to-all(f32[16,16,128]{2,1,0:T(8,128)S(1)} %broadcast_in_dim.6), channel_id=1, replica_groups=mesh['z'=8,'y'=8,'core'=2,'term'=4] {'z','core'}, dimensions={0} | all-to-all | bytes 262144 | tf_op jit(solution)/shard_map/all_to_all | solution.py:135
  96.3 15.7 %all_to_all.28 = f32[32,16,128]{2,1,0:T(8,128)S(1)} all-to-all(f32[32,16,128]{2,1,0:T(8,128)S(1)} %broadcast_in_dim.7), channel_id=1, replica_groups=mesh['z'=8,'y'=8,'core'=2,'term'=4] {'y','term'}, dimensions={0} | all-to-all | bytes 524288 | tf_op jit(solution)/shard_map/all_to_all | solution.py:135
  112.0 0.0 copy-done.2
  112.0 54.2 %shard_map.79 = (f32[128,256]{1,0:T(8,128)}, bf16[2048,256]{1,0:T(8,128)(2,1)}, f32[1,256]{1,0:T(1,128)}) custom-call(f32[256,256]{1,0:T(8,128)S(1)} %pad_maximum_fusion.1.window_ref, f32[1,256]{1,0:T(1,128)S(1)} %bitcast.28, f32[128,256]{1,0:T(8,128)S(1)} %reduce_sum.27.share_ref, bf16[2048,256]{1,0:T(8,128)(2,1)S(1)} %bitcast.23), custom_call_target="tpu_custom_call" | custom-call | tf_op jit(solution)/shard_map/pallas_call | solution.py:149
  (9 shorter events, 0.2 us)
Async XLA Ops:
  4.5 40.4 %all-to-all-start = ((f32[128,1,1152]{2,1,0:T(1,128)}), f32[128,1,1152]{2,1,0:T(1,128)S(1)}, u32[]{:S(2)}, u32[]{:S(2)}) async-start(f32[128,1,1152]{2,1,0:T(1,128)} %bitcast.30), calls=%async_computation | async-start | bytes 1179648 | tf_op jit(solution)/shard_map/all_to_all | solution.py:135
  45.9 5.0 %copy-start = (bf16[1,2048,256]{2,1,0:T(8,128)(2,1)S(1)}, bf16[1,2048,256]{2,1,0:T(8,128)(2,1)}, u32[]{:S(2)}) copy-start(bf16[1,2048,256]{2,1,0:T(8,128)(2,1)} %param.8) | copy-start | bytes 3145732
  46.0 5.0 %copy-start.1 = (f32[1,16,4]{1,2,0:T(4,128)S(1)}, f32[1,16,4]{1,2,0:T(4,128)}, u32[]{:S(2)}) copy-start(f32[1,16,4]{1,2,0:T(4,128)} %param.6) | copy-start | bytes 772
  46.0 5.0 %collective-permute-start = (f32[16,64]{1,0:T(8,128)S(1)}, f32[16,64]{1,0:T(8,128)S(1)}, u32[]{:S(2)}, u32[]{:S(2)}) collective-permute-start(f32[16,64]{1,0:T(8,128)S(1)} %get-tuple-element.9), channel_id=1, source_target_pairs={{0,4},{4,0},{1,5},{5,1},{2,6},{6,2},{3,7},{7,3},{8,12},{12,8},{9,1... | collective-permute-start | bytes 12296 | tf_op jit(solution)/shard_map/ppermute | solution.py:143
  65.6 46.5 %copy-start.2 = (f32[256]{0:T(256)S(1)}, f32[256]{0:T(256)}, u32[]{:S(2)}) copy-start(f32[256]{0:T(256)} %param.9) | copy-start | bytes 3076

commit v3 on v2

--- a/solution.py
+++ b/solution.py
@@ -50,17 +50,40 @@
     return jnp.concatenate([tile * root for tile in tiles], axis=1)
 
 
+def split(value):
+    high = value.astype(jnp.bfloat16)
+    rest = value - high.astype(jnp.float32)
+    middle = rest.astype(jnp.bfloat16)
+    return high, middle, (rest - middle.astype(jnp.float32)).astype(jnp.bfloat16)
+
+
+def fold(rows, second):
+    high, middle, low = split(rows)
+    right = jnp.concatenate([high, middle, high, middle, low, high], axis=0)
+    left = jnp.concatenate([high, high, middle, middle, high, low], axis=0)
+    return lax.dot_general(
+        left[:, second : second + PANEL],
+        right,
+        (((0,), (0,)), ((), ())),
+        preferred_element_type=jnp.float32,
+    )
+
+
 def orthonormal_rows(work):
     size = work.shape[0]
     for outer in range(0, size, OUTER):
-        end = outer + OUTER
+        end = min(outer + OUTER, size)
+        panel = work[outer : outer + PANEL, :]
         for first in range(outer, end, PANEL):
-            panel = work[first : first + PANEL, :]
-            if first > outer:
-                panel = panel - contract(
-                    work[outer:first, first : first + PANEL], work[outer:first, :], 0, 0
-                )
-            work[first : first + PANEL, :] = eliminate(panel, first)
+            second = first + PANEL
+            if second < end:
+                ahead = work[second : second + PANEL, :]
+                if first > outer:
+                    ahead = ahead - contract(work[outer:first, second : second + PANEL], work[outer:first, :], 0, 0)
+            rows = eliminate(panel, first)
+            work[first:second, :] = rows
+            if second < end:
+                panel = ahead - fold(rows, second)
         if end < size:
             work[end:, :] = work[end:, :] - contract(work[outer:end, end:size], work[outer:end, :], 0, 0)
 
@@ -213,7 +236,7 @@
 def mass_pieces(counts, scales, block_ids, doc_count):
     height, docs = counts.shape
     stored = block_ids.shape[0]
-    steps = 4
+    steps = 2
     return pl.pallas_call(
         functools.partial(mass_pieces_kernel, stored // steps),
         grid=(steps,),
@@ -229,7 +252,30 @@
     )(counts, scales.T, block_ids.reshape(1, stored))
 
 
-def find_masses_kernel(stored, place_ref, incoming_ref, keep_ref, send_ref):
+def turn_kernel(after_ref, counts_ref, turned_ref):
+    turned_ref[...] = counts_ref[...].T
+
+
+def turn(counts, after):
+    height, docs = counts.shape
+    steps = 4
+    return pl.pallas_call(
+        turn_kernel,
+        grid=(steps,),
+        in_specs=[
+            pl.BlockSpec(memory_space=pl.ANY),
+            pl.BlockSpec((height // steps, docs), lambda i: (i, 0)),
+        ],
+        out_specs=pl.BlockSpec((docs, height // steps), lambda i: (0, i)),
+        out_shape=jax.ShapeDtypeStruct((docs, height), counts.dtype),
+        compiler_params=pltpu.CompilerParams(vmem_limit_bytes=16 * 2**20),
+        cost_estimate=pl.CostEstimate(
+            flops=0, bytes_accessed=4 * height * docs, transcendentals=0
+        ),
+    )(after, counts)
+
+
+def find_masses_kernel(stored, place_ref, incoming_ref, before_ref, keep_ref, send_ref):
     piece = stored // 2 + 1
     batches = incoming_ref.shape[0] // piece
     half = LANES // 2
@@ -267,18 +313,19 @@
     send_ref[...] = jnp.where(mine, masses[stored:], masses[:stored])
 
 
-def find_masses(incoming, chip, core, stored):
+def find_masses(incoming, before, chip, core, stored):
     shape = jax.ShapeDtypeStruct((stored, LANES // 2), jnp.float32)
     return pl.pallas_call(
         functools.partial(find_masses_kernel, stored),
         in_specs=[
             pl.BlockSpec(memory_space=pltpu.SMEM),
             pl.BlockSpec(memory_space=pltpu.VMEM),
+            pl.BlockSpec(memory_space=pl.ANY),
         ],
         out_specs=(pl.BlockSpec(memory_space=pltpu.VMEM), pl.BlockSpec(memory_space=pltpu.VMEM)),
         out_shape=(shape, shape),
         compiler_params=pltpu.CompilerParams(vmem_limit_bytes=16 * 2**20),
-    )(jnp.stack([chip, core]).astype(jnp.int32), incoming)
+    )(jnp.stack([chip, core]).astype(jnp.int32), incoming, before)
 
 
 def project_kernel(
@@ -339,10 +386,10 @@
     share_docs = batch_docs // term_count
     pieces = mass_pieces(counts, scales, block_ids, doc_count)
     incoming = all_to_all(pieces.reshape(doc_count, 1, -1), ("z", "y", "core"))
-    turned = counts.T
+    turned = turn(counts, pieces[:8])
     chip = lax.axis_index("z") * lines + lax.axis_index("y")
     core = lax.axis_index("core")
-    keep, send = find_masses(incoming.reshape(-1, LANES), chip, core, stored_blocks)
+    keep, send = find_masses(incoming.reshape(-1, LANES), turned, chip, core, stored_blocks)
     come = swap_cores(send)
     partial = project(core, keep, come, scales, basis_rows, turned, total_docs)
     partial = partial.reshape(term_count, share_docs, rank_size)

time: 167 us -> 159 us (0.952)
  Pallas kernels: 60.9 us -> 56.8 us
  waiting for transfers between devices: 21.9 us -> 19.5 us
    pallas_call x1, Pallas kernels: 54.2 us -> 49.5 us  [finish(): pl.pallas_call(rotate, in_specs=[pl.BlockSpec(memory_space=pltpu.VMEM)] *...]
    all_to_all x1, waiting for transfers between devices: 21.9 us -> 18.3 us  [all_to_all(): return lax.all_to_all(pieces, axes, 0, 0, tiled=True)]
  transfers between devices with their start and end apart: 2 -> 2, of which waited for: 1 -> 2; matrix products, arithmetic and copies ran while one was open for 2% -> 0% of each run, Pallas kernels for 0% -> 1%
where the time goes in v3:
time: 159 us
  blocking collectives  57.7 us (36%)
  Pallas kernels  56.8 us (36%)
  starting transfers between devices  20.7 us (13%)
  waiting for transfers between devices  19.5 us (12%)
  local copies, waits for them, and re-layouts  2.37 us (1%)
    all_to_all x4, blocking collectives, all_to_all(): return lax.all_to_all(pieces, axes, 0, 0, tiled=True)  57.7 us
    pallas_call x1, Pallas kernels, finish(): pl.pallas_call(rotate, in_specs=[pl.BlockSpec(memory_space=pltpu.VMEM)] *...  49.5 us
    all_to_all x1, starting transfers between devices, all_to_all(): return lax.all_to_all(pieces, axes, 0, 0, tiled=True)  18.8 us
    all_to_all x1, waiting for transfers between devices, all_to_all(): return lax.all_to_all(pieces, axes, 0, 0, tiled=True)  18.3 us
  transfers between devices with their start and end apart: 2, of which 2 were waited for; matrix products, arithmetic and copies ran while one was open for 0% of the time, Pallas kernels for 1%

profile of v3, /device:TPU:1, one launch (start us, length us, event | category | flops | bytes accessed | tf_op | source)
XLA Modules:
  0.0 158.6 jit_solution(153693468705073964)
XLA Ops:
  0.6 3.0 %shard_map.76 = f32[1152,128]{1,0:T(8,128)} custom-call(bf16[2048,512]{1,0:T(8,128)(2,1)} %bitcast.18, f32[4,16]{1,0:T(4,128)} %bitcast.23, s32[1,16]{1,0:T(1,128)} %ids_ref.1), custom_call_target="tpu_custom_call" | custom-call | tf_op jit(solution)/shard_map/pallas_call | solution.py:240
  3.6 18.8 %all-to-all-start = ((f32[128,1,1152]{2,1,0:T(1,128)}), f32[128,1,1152]{2,1,0:T(1,128)}, u32[]{:S(2)}, u32[]{:S(2)}) async-start(f32[128,1,1152]{2,1,0:T(1,128)} %bitcast.26), calls=%async_computation | async-start | bytes 1179648 | tf_op jit(solution)/shard_map/all_to_all | solution.py:158
  22.4 0.7 slice.28.after_ref
  23.1 0.0 copy-start
  23.1 1.6 %copy-done = bf16[1,2048,512]{2,1,0:T(8,128)(2,1)S(1)} copy-done((bf16[1,2048,512]{2,1,0:T(8,128)(2,1)S(1)}, bf16[1,2048,512]{2,1,0:T(8,128)(2,1)}, u32[]{:S(2)}) %copy-start) | copy-done | bytes 2097176
  24.7 0.9 shard_map.77.before_ref.turned_ref
  25.6 0.0 copy-start.1
  25.7 0.0 copy-start.2
  25.7 0.1 pad_add_fusion.place_ref
  25.8 18.3 %all-to-all-done = f32[128,1,1152]{2,1,0:T(1,128)} async-done(((f32[128,1,1152]{2,1,0:T(1,128)}), f32[128,1,1152]{2,1,0:T(1,128)}, u32[]{:S(2)}, u32[]{:S(2)}) %all-to-all-start) | async-done | bytes 589856 | tf_op jit(solution)/shard_map/all_to_all | solution.py:158
  44.1 1.6 %shard_map.78 = (f32[16,64]{1,0:T(8,128)S(1)}, f32[16,64]{1,0:T(8,128)S(1)}) custom-call(s32[2]{0:T(128)S(1)} %pad_add_fusion.place_ref, f32[1152,128]{1,0:T(8,128)} %bitcast.6.incoming_ref, bf16[512,2048]{1,0:T(8,128)(2,1)S(1)} %shard_map.77.before_ref.turned_ref), custom_call_target="tpu_custom_call" | custom-call | tf_op jit(solution)/shard_map/pallas_call | solution.py:318
  45.7 1.9 %collective-permute-start = (f32[16,64]{1,0:T(8,128)S(1)}, f32[16,64]{1,0:T(8,128)S(1)}, u32[]{:S(2)}, u32[]{:S(2)}) collective-permute-start(f32[16,64]{1,0:T(8,128)S(1)} %get-tuple-element.9), channel_id=1, source_target_pairs={{0,4},{4,0},{1,5},{5,1},{2,6},{6,2},{3,7},{7,3},{8,12},{12,8},{9,1... | collective-permute-start | bytes 12296 | tf_op jit(solution)/shard_map/ppermute | solution.py:166
  47.6 1.1 collective-permute-done.come_ref
  48.8 0.0 copy-done.1
  48.8 0.0 copy-done.2
  48.8 1.7 %shard_map.79 = f32[512,256]{1,0:T(8,128)S(1)} custom-call(s32[1]{0:T(128)} %bitcast.core_ref, f32[16,64]{1,0:T(8,128)S(1)} %get-tuple-element.8.keep_ref, f32[16,64]{1,0:T(8,128)S(1)} %collective-permute-done.come_ref, f32[4,16]{1,0:T(4,128)S(1)} %bitcast.24, bf16[2048,256]{1,0:T(8,128)(2,1)S(1)} %bitcast.20, ...), custom_call_target="tpu_custom_call" | custom-call | tf_op jit(solution)/shard_map/pallas_call | solution.py:364
  50.5 13.0 %all_to_all.25 = f32[4,128,256]{2,1,0:T(8,128)S(1)} all-to-all(f32[4,128,256]{2,1,0:T(8,128)S(1)} %bitcast.22), channel_id=1, replica_groups=mesh['z'=8,'y'=8,'core'=2,'term'=4] {'term'}, dimensions={0} | all-to-all | bytes 1048576 | tf_op jit(solution)/shard_map/all_to_all | solution.py:158
  63.5 0.4 convolution_multiply_fusion
  63.9 0.0 copy-start.3
  64.0 14.0 %all_to_all.26 = f32[32,16,128]{2,1,0:T(8,128)S(1)} all-to-all(f32[32,16,128]{2,1,0:T(8,128)S(1)} %bitcast.27), channel_id=1, replica_groups=mesh['z'=8,'y'=8,'core'=2,'term'=4] {'y','term'}, dimensions={0} | all-to-all | bytes 524288 | tf_op jit(solution)/shard_map/all_to_all | solution.py:158
  78.0 15.4 %all_to_all.27 = f32[16,16,128]{2,1,0:T(8,128)S(1)} all-to-all(f32[16,16,128]{2,1,0:T(8,128)S(1)} %broadcast_in_dim.6), channel_id=1, replica_groups=mesh['z'=8,'y'=8,'core'=2,'term'=4] {'z','core'}, dimensions={0} | all-to-all | bytes 262144 | tf_op jit(solution)/shard_map/all_to_all | solution.py:158
  93.5 15.4 %all_to_all.28 = f32[32,16,128]{2,1,0:T(8,128)S(1)} all-to-all(f32[32,16,128]{2,1,0:T(8,128)S(1)} %broadcast_in_dim.7), channel_id=1, replica_groups=mesh['z'=8,'y'=8,'core'=2,'term'=4] {'y','term'}, dimensions={0} | all-to-all | bytes 524288 | tf_op jit(solution)/shard_map/all_to_all | solution.py:158
  108.9 0.0 copy-done.3
  108.9 49.5 %shard_map.80 = (f32[128,256]{1,0:T(8,128)}, bf16[2048,256]{1,0:T(8,128)(2,1)}, f32[1,256]{1,0:T(1,128)}) custom-call(f32[256,256]{1,0:T(8,128)S(1)} %pad_maximum_fusion.1.window_ref, f32[1,256]{1,0:T(1,128)S(1)} %bitcast.25, f32[128,256]{1,0:T(8,128)S(1)} %reduce_sum.27.share_ref, bf16[2048,256]{1,0:T(8,128)(2,1)S(1)} %bitcast.21), custom_call_target="tpu_custom_call" | custom-call | tf_op jit(solution)/shard_map/pallas_call | solution.py:172
  (9 shorter events, 0.2 us)
Async XLA Ops:
  3.6 40.5 %all-to-all-start = ((f32[128,1,1152]{2,1,0:T(1,128)}), f32[128,1,1152]{2,1,0:T(1,128)}, u32[]{:S(2)}, u32[]{:S(2)}) async-start(f32[128,1,1152]{2,1,0:T(1,128)} %bitcast.26), calls=%async_computation | async-start | bytes 1179648 | tf_op jit(solution)/shard_map/all_to_all | solution.py:158
  23.1 1.6 %copy-start = (bf16[1,2048,512]{2,1,0:T(8,128)(2,1)S(1)}, bf16[1,2048,512]{2,1,0:T(8,128)(2,1)}, u32[]{:S(2)}) copy-start(bf16[1,2048,512]{2,1,0:T(8,128)(2,1)} %param.5) | copy-start | bytes 6291460
  25.6 23.1 %copy-start.1 = (bf16[1,2048,256]{2,1,0:T(8,128)(2,1)S(1)}, bf16[1,2048,256]{2,1,0:T(8,128)(2,1)}, u32[]{:S(2)}) copy-start(bf16[1,2048,256]{2,1,0:T(8,128)(2,1)} %param.8) | copy-start | bytes 3145732
  25.7 23.1 %copy-start.2 = (f32[1,16,4]{1,2,0:T(4,128)S(1)}, f32[1,16,4]{1,2,0:T(4,128)}, u32[]{:S(2)}) copy-start(f32[1,16,4]{1,2,0:T(4,128)} %param.6) | copy-start | bytes 772
  45.7 3.1 %collective-permute-start = (f32[16,64]{1,0:T(8,128)S(1)}, f32[16,64]{1,0:T(8,128)S(1)}, u32[]{:S(2)}, u32[]{:S(2)}) collective-permute-start(f32[16,64]{1,0:T(8,128)S(1)} %get-tuple-element.9), channel_id=1, source_target_pairs={{0,4},{4,0},{1,5},{5,1},{2,6},{6,2},{3,7},{7,3},{8,12},{12,8},{9,1... | collective-permute-start | bytes 12296 | tf_op jit(solution)/shard_map/ppermute | solution.py:166
  63.9 45.0 %copy-start.3 = (f32[256]{0:T(256)S(1)}, f32[256]{0:T(256)}, u32[]{:S(2)}) copy-start(f32[256]{0:T(256)} %param.9) | copy-start | bytes 3076

commit v4 on v3

--- a/solution.py
+++ b/solution.py
@@ -12,8 +12,9 @@
 TERMS = 131072
 ITERS = 4
 LANES = 128
-PANEL = 16
-OUTER = 128
+PANEL = 32
+HALF = 16
+OUTER = 256
 
 
 forget_factor = 0.85
@@ -31,23 +32,42 @@
 
 
 def eliminate(panel, first):
-    size = panel.shape[0]
-    rows = lax.broadcasted_iota(jnp.int32, (size, LANES), 0)
-    columns = [
-        jnp.broadcast_to(panel[:, first + k : first + k + 1], (size, LANES)) for k in range(size)
+    height = panel.shape[0]
+    rows = lax.broadcasted_iota(jnp.int32, (HALF, LANES), 0)
+    parts = [
+        [panel[top : top + HALF, t : t + LANES] for t in range(0, panel.shape[1], LANES)]
+        for top in range(0, height, HALF)
     ]
-    tiles = [panel[:, t : t + LANES] for t in range(0, panel.shape[1], LANES)]
-    pivots = jnp.zeros((size, LANES), jnp.float32)
-    for k in range(size):
-        pivot = columns[k][k : k + 1, :]
-        pivots = jnp.where(rows == k, jnp.broadcast_to(pivot, (size, LANES)), pivots)
-        if k + 1 < size:
-            factor = jnp.where(rows > k, columns[k] * (1.0 / pivot), 0.0)
-            for m in range(k + 1, size):
-                columns[m] = columns[m] - factor * columns[m][k : k + 1, :]
-            tiles = [tile - factor * tile[k : k + 1, :] for tile in tiles]
-    root = lax.rsqrt(pivots)
-    return jnp.concatenate([tile * root for tile in tiles], axis=1)
+    done = []
+    while parts:
+        lead, *below = parts
+        start = first + len(done) * HALF
+        tile, lane = start // LANES, start % LANES
+        columns = [
+            [jnp.broadcast_to(part[tile][:, lane + k : lane + k + 1], (HALF, LANES)) for k in range(HALF)]
+            for part in parts
+        ]
+        pivots = jnp.zeros((HALF, LANES), jnp.float32)
+        for k in range(HALF):
+            pivot = columns[0][k][k : k + 1, :]
+            pivots = jnp.where(rows == k, jnp.broadcast_to(pivot, (HALF, LANES)), pivots)
+            unit = 1.0 / pivot
+            factors = [jnp.where(rows > k, columns[0][k] * unit, 0.0)]
+            factors += [column[k] * unit for column in columns[1:]]
+            for m in range(k + 1, HALF):
+                value = columns[0][m][k : k + 1, :]
+                for column, factor in zip(columns, factors):
+                    column[m] = column[m] - factor * value
+            values = [entry[k : k + 1, :] for entry in lead]
+            lead = [entry - factors[0] * value for entry, value in zip(lead, values)]
+            below = [
+                [entry - factor * value for entry, value in zip(part, values)]
+                for part, factor in zip(below, factors[1:])
+            ]
+        root = lax.rsqrt(pivots)
+        done.append(jnp.concatenate([entry * root for entry in lead], axis=1))
+        parts = below
+    return jnp.concatenate(done, axis=0)
 
 
 def split(value):
@@ -95,18 +115,68 @@
     orthonormal_rows(work)
 
 
+def pack(matrix):
+    half = LANES // 2
+    lower = lax.broadcasted_iota(jnp.int32, (half, LANES), 1) < half
+    inner = pltpu.roll(matrix[half:LANES, :LANES], half, 1)
+    corner = matrix[LANES + half :, LANES:]
+    return jnp.concatenate(
+        [
+            matrix[:half, :LANES],
+            matrix[:half, LANES:],
+            matrix[half:LANES, LANES:],
+            matrix[LANES : LANES + half, LANES:],
+            jnp.where(lower, inner, corner),
+        ],
+        axis=0,
+    )
+
+
+def unpack(packed):
+    half = LANES // 2
+    blocks = [packed[top : top + half] for top in range(0, packed.shape[0], half)]
+    spare = jnp.zeros((half, LANES), jnp.float32)
+    left = jnp.concatenate([blocks[0], pltpu.roll(blocks[4], half, 1), spare, spare], axis=0)
+    right = jnp.concatenate([blocks[1], blocks[2], blocks[3], blocks[4]], axis=0)
+    upper = jnp.concatenate([left, right], axis=1)
+    row = lax.broadcasted_iota(jnp.int32, upper.shape, 0) // half
+    column = lax.broadcasted_iota(jnp.int32, upper.shape, 1) // half
+    return jnp.where(row <= column, upper, upper.T)
+
+
+def own_gram_kernel(total_docs, incoming_ref, share_ref, packed_ref):
+    share = jnp.sum(incoming_ref[...], axis=0)
+    share_ref[...] = share
+    packed_ref[...] = pack(contract(share, share, 0, 0) * (1.0 / total_docs))
+
+
+def own_gram(incoming, total_docs):
+    docs, rank_size = incoming.shape[1:]
+    vmem = pl.BlockSpec(memory_space=pltpu.VMEM)
+    return pl.pallas_call(
+        functools.partial(own_gram_kernel, total_docs),
+        in_specs=[vmem],
+        out_specs=(vmem, vmem),
+        out_shape=(
+            jax.ShapeDtypeStruct((docs, rank_size), jnp.float32),
+            jax.ShapeDtypeStruct((5 * LANES // 2, LANES), jnp.float32),
+        ),
+        compiler_params=pltpu.CompilerParams(vmem_limit_bytes=8 * 2**20),
+    )(incoming)
+
+
 def rotate(
-    window_ref, sv_ref, share_ref, prior_hbm,
+    packed_ref, sv_ref, share_ref, prior_hbm,
     coords_ref, rows_hbm, singular_ref,
     gram, work, rotation, prior, rows, load, store,
 ):
     loading = pltpu.make_async_copy(prior_hbm, prior, load)
     loading.start()
-    size = window_ref.shape[0]
+    size = sv_ref.shape[1]
     row = lax.broadcasted_iota(jnp.int32, (size, size), 0)
     column = lax.broadcasted_iota(jnp.int32, (size, size), 1)
     sv = sv_ref[...]
-    whole = window_ref[...] + jnp.where(row == column, forget_factor * sv * sv, 0.0)
+    whole = unpack(packed_ref[...]) + jnp.where(row == column, forget_factor * sv * sv, 0.0)
     gram[...] = whole
     diagonal = jnp.where(row == column, whole, 0.0)
     top = jnp.max(jnp.max(diagonal, axis=0, keepdims=True), axis=1, keepdims=True)
@@ -166,7 +236,7 @@
     return lax.ppermute(array, "core", [(0, 1), (1, 0)])
 
 
-def finish(window, prior_sv, share_rows, basis_rows):
+def finish(packed, prior_sv, share_rows, basis_rows):
     height, rank_size = basis_rows.shape
     parts = 4
     return pl.pallas_call(
@@ -192,7 +262,7 @@
             pltpu.SemaphoreType.DMA((parts,)),
         ],
         compiler_params=pltpu.CompilerParams(vmem_limit_bytes=32 * 2**20),
-    )(window, prior_sv.reshape(1, rank_size), share_rows, basis_rows)
+    )(packed, prior_sv.reshape(1, rank_size), share_rows, basis_rows)
 
 
 def mass_pieces_kernel(slots, counts_ref, scale_ref, ids_ref, pieces_ref, mass):
@@ -268,7 +338,7 @@
         ],
         out_specs=pl.BlockSpec((docs, height // steps), lambda i: (0, i)),
         out_shape=jax.ShapeDtypeStruct((docs, height), counts.dtype),
-        compiler_params=pltpu.CompilerParams(vmem_limit_bytes=16 * 2**20),
+        compiler_params=pltpu.CompilerParams(vmem_limit_bytes=6 * 2**20),
         cost_estimate=pl.CostEstimate(
             flops=0, bytes_accessed=4 * height * docs, transcendentals=0
         ),
@@ -324,7 +394,7 @@
         ],
         out_specs=(pl.BlockSpec(memory_space=pltpu.VMEM), pl.BlockSpec(memory_space=pltpu.VMEM)),
         out_shape=(shape, shape),
-        compiler_params=pltpu.CompilerParams(vmem_limit_bytes=16 * 2**20),
+        compiler_params=pltpu.CompilerParams(vmem_limit_bytes=6 * 2**20),
     )(jnp.stack([chip, core]).astype(jnp.int32), incoming, before)
 
 
@@ -393,19 +463,14 @@
     come = swap_cores(send)
     partial = project(core, keep, come, scales, basis_rows, turned, total_docs)
     partial = partial.reshape(term_count, share_docs, rank_size)
-    share_rows = jnp.sum(all_to_all(partial, "term"), axis=0)
-    own_gram = jnp.dot(share_rows.T, share_rows, precision=highest) / total_docs
-    flat_gram = jnp.concatenate([own_gram[:, t : t + LANES] for t in range(0, rank_size, LANES)])
+    share_rows, packed = own_gram(all_to_all(partial, "term"), total_docs)
     plane = ("y", "term")
     across = ("z", "core")
     plane_count = lines * term_count
-    plane_gram = jnp.sum(all_to_all(flat_gram.reshape(plane_count, -1, LANES), plane), axis=0)
+    plane_gram = jnp.sum(all_to_all(packed.reshape(plane_count, 1, -1), plane), axis=0)
     piece_gram = jnp.sum(all_to_all(repeat(plane_gram, doc_count // lines), across), axis=0)
-    flat_gram = all_to_all(repeat(piece_gram, plane_count), plane).reshape(-1, LANES)
-    window = jnp.concatenate(
-        [flat_gram[t : t + rank_size] for t in range(0, flat_gram.shape[0], rank_size)], axis=1
-    )
-    doc_coords, new_rows, singular = finish(window, prior_sv, share_rows, basis_rows)
+    packed = all_to_all(repeat(piece_gram, plane_count), plane).reshape(-1, LANES)
+    doc_coords, new_rows, singular = finish(packed, prior_sv, share_rows, basis_rows)
     return (doc_coords, new_rows[None], singular.reshape(rank_size))
 
 

time: 159 us -> 147 us (0.925)
  Pallas kernels: 56.8 us -> 49.8 us
  blocking collectives: 57.7 us -> 53 us
    pallas_call x1, Pallas kernels: 49.5 us -> 42.1 us  [finish(): pl.pallas_call(rotate, in_specs=[pl.BlockSpec(memory_space=pltpu.VMEM)] *...]
    all_to_all x4, blocking collectives: 57.7 us -> 53 us  [all_to_all(): return lax.all_to_all(pieces, axes, 0, 0, tiled=True)]
  transfers between devices with their start and end apart: 2 -> 2, of which waited for: 2 -> 2; matrix products, arithmetic and copies ran while one was open for 0% -> 1% of each run, Pallas kernels for 1% -> 1%
where the time goes in v4:
time: 147 us
  blocking collectives  53 us (36%)
  Pallas kernels  49.8 us (34%)
  starting transfers between devices  20.7 us (14%)
  waiting for transfers between devices  19.5 us (13%)
  local copies, waits for them, and re-layouts  2.43 us (2%)
    all_to_all x4, blocking collectives, all_to_all(): return lax.all_to_all(pieces, axes, 0, 0, tiled=True)  53 us
    pallas_call x1, Pallas kernels, finish(): pl.pallas_call(rotate, in_specs=[pl.BlockSpec(memory_space=pltpu.VMEM)] *...  42.1 us
    all_to_all x1, starting transfers between devices, all_to_all(): return lax.all_to_all(pieces, axes, 0, 0, tiled=True)  18.8 us
    all_to_all x1, waiting for transfers between devices, all_to_all(): return lax.all_to_all(pieces, axes, 0, 0, tiled=True)  18.3 us
    pallas_call x1, Pallas kernels, mass_pieces(): pl.pallas_call(functools.partial(mass_pieces_kernel, stored // steps), gr...  2.98 us
  transfers between devices with their start and end apart: 2, of which 2 were waited for; matrix products, arithmetic and copies ran while one was open for 1% of the time, Pallas kernels for 1%

profile of v4, /device:TPU:1, one launch (start us, length us, event | category | flops | bytes accessed | tf_op | source)
XLA Modules:
  0.0 146.6 jit_solution(8042791700528484479)
XLA Ops:
  0.6 3.0 %shard_map.76 = f32[1152,128]{1,0:T(8,128)} custom-call(bf16[2048,512]{1,0:T(8,128)(2,1)} %bitcast.15, f32[4,16]{1,0:T(4,128)} %bitcast.22, s32[1,16]{1,0:T(1,128)} %ids_ref.1), custom_call_target="tpu_custom_call" | custom-call | tf_op jit(solution)/shard_map/pallas_call | solution.py:310
  3.6 18.8 %all-to-all-start = ((f32[128,1,1152]{2,1,0:T(1,128)}), f32[128,1,1152]{2,1,0:T(1,128)}, u32[]{:S(2)}, u32[]{:S(2)}) async-start(f32[128,1,1152]{2,1,0:T(1,128)} %bitcast.25), calls=%async_computation | async-start | bytes 1179648 | tf_op jit(solution)/shard_map/all_to_all | solution.py:228
  22.4 0.7 slice.4.after_ref
  23.1 0.0 copy-start
  23.1 1.6 %copy-done = bf16[1,2048,512]{2,1,0:T(8,128)(2,1)S(1)} copy-done((bf16[1,2048,512]{2,1,0:T(8,128)(2,1)S(1)}, bf16[1,2048,512]{2,1,0:T(8,128)(2,1)}, u32[]{:S(2)}) %copy-start) | copy-done | bytes 2097176
  24.7 0.9 shard_map.77.before_ref.turned_ref
  25.6 0.0 copy-start.1
  25.7 0.0 copy-start.2
  25.7 0.1 pad_add_fusion.place_ref
  25.8 18.3 %all-to-all-done = f32[128,1,1152]{2,1,0:T(1,128)} async-done(((f32[128,1,1152]{2,1,0:T(1,128)}), f32[128,1,1152]{2,1,0:T(1,128)}, u32[]{:S(2)}, u32[]{:S(2)}) %all-to-all-start) | async-done | bytes 589856 | tf_op jit(solution)/shard_map/all_to_all | solution.py:228
  44.1 1.6 %shard_map.78 = (f32[16,64]{1,0:T(8,128)S(1)}, f32[16,64]{1,0:T(8,128)S(1)}) custom-call(s32[2]{0:T(128)S(1)} %pad_add_fusion.place_ref, f32[1152,128]{1,0:T(8,128)} %bitcast.6.incoming_ref, bf16[512,2048]{1,0:T(8,128)(2,1)S(1)} %shard_map.77.before_ref.turned_ref), custom_call_target="tpu_custom_call" | custom-call | tf_op jit(solution)/shard_map/pallas_call | solution.py:388
  45.7 1.9 %collective-permute-start = (f32[16,64]{1,0:T(8,128)S(1)}, f32[16,64]{1,0:T(8,128)S(1)}, u32[]{:S(2)}, u32[]{:S(2)}) collective-permute-start(f32[16,64]{1,0:T(8,128)S(1)} %get-tuple-element.11), channel_id=1, source_target_pairs={{0,4},{4,0},{1,5},{5,1},{2,6},{6,2},{3,7},{7,3},{8,12},{12,8},{9,1... | collective-permute-start | bytes 12296 | tf_op jit(solution)/shard_map/ppermute | solution.py:236
  47.6 1.1 collective-permute-done.come_ref
  48.8 0.0 copy-done.1
  48.8 0.0 copy-done.2
  48.8 1.7 %shard_map.79 = f32[512,256]{1,0:T(8,128)S(1)} custom-call(s32[1]{0:T(128)} %bitcast.core_ref, f32[16,64]{1,0:T(8,128)S(1)} %get-tuple-element.10.keep_ref, f32[16,64]{1,0:T(8,128)S(1)} %collective-permute-done.come_ref, f32[4,16]{1,0:T(4,128)S(1)} %bitcast.23, bf16[2048,256]{1,0:T(8,128)(2,1)S(1)} %bitcast.17, ...), custom_call_target="tpu_custom_call" | custom-call | tf_op jit(solution)/shard_map/pallas_call | solution.py:434
  50.5 0.0 copy-start.3
  50.5 13.0 %all_to_all.25.incoming_ref = f32[4,128,256]{2,1,0:T(8,128)S(1)} all-to-all(f32[4,128,256]{2,1,0:T(8,128)S(1)} %bitcast.19), channel_id=1, replica_groups=mesh['z'=8,'y'=8,'core'=2,'term'=4] {'term'}, dimensions={0} | all-to-all | bytes 1048576 | tf_op jit(solution)/shard_map/all_to_all | solution.py:228
  63.5 0.5 shard_map.80
  63.9 13.2 %all_to_all.26 = f32[32,1,1280]{2,1,0:T(1,128)S(1)} all-to-all(f32[32,1,1280]{2,1,0:T(1,128)S(1)} %bitcast.21), channel_id=1, replica_groups=mesh['z'=8,'y'=8,'core'=2,'term'=4] {'y','term'}, dimensions={0} | all-to-all | bytes 327680 | tf_op jit(solution)/shard_map/all_to_all | solution.py:228
  77.1 0.1 reduce_sum.18
  77.3 13.8 %all_to_all.27 = f32[16,1,1280]{2,1,0:T(1,128)S(1)} all-to-all(f32[16,1,1280]{2,1,0:T(1,128)S(1)} %broadcast_in_dim.6), channel_id=1, replica_groups=mesh['z'=8,'y'=8,'core'=2,'term'=4] {'z','core'}, dimensions={0} | all-to-all | bytes 163840 | tf_op jit(solution)/shard_map/all_to_all | solution.py:228
  91.1 0.1 reduce_sum.19
  91.1 0.1 broadcast_in_dim.7
  91.2 13.1 %all_to_all.28 = f32[32,1,1280]{2,1,0:T(1,128)S(1)} all-to-all(f32[32,1,1280]{2,1,0:T(1,128)S(1)} %broadcast_in_dim.7), channel_id=1, replica_groups=mesh['z'=8,'y'=8,'core'=2,'term'=4] {'y','term'}, dimensions={0} | all-to-all | bytes 327680 | tf_op jit(solution)/shard_map/all_to_all | solution.py:228
  104.3 0.0 copy-done.3
  104.3 42.1 %shard_map.81 = (f32[128,256]{1,0:T(8,128)}, bf16[2048,256]{1,0:T(8,128)(2,1)}, f32[1,256]{1,0:T(1,128)}) custom-call(f32[320,128]{1,0:T(8,128)S(1)} %bitcast.20, f32[1,256]{1,0:T(1,128)S(1)} %bitcast.24, f32[128,256]{1,0:T(8,128)S(1)} %get-tuple-element.13.share_ref, bf16[2048,256]{1,0:T(8,128)(2,1)S(1)} %bitcast.18), custom_call_target="tpu_custom_call" | custom-call | tf_op jit(solution)/shard_map/pallas_call | solution.py:242
  (1 shorter events, 0.0 us)
Async XLA Ops:
  3.6 40.5 %all-to-all-start = ((f32[128,1,1152]{2,1,0:T(1,128)}), f32[128,1,1152]{2,1,0:T(1,128)}, u32[]{:S(2)}, u32[]{:S(2)}) async-start(f32[128,1,1152]{2,1,0:T(1,128)} %bitcast.25), calls=%async_computation | async-start | bytes 1179648 | tf_op jit(solution)/shard_map/all_to_all | solution.py:228
  23.1 1.6 %copy-start = (bf16[1,2048,512]{2,1,0:T(8,128)(2,1)S(1)}, bf16[1,2048,512]{2,1,0:T(8,128)(2,1)}, u32[]{:S(2)}) copy-start(bf16[1,2048,512]{2,1,0:T(8,128)(2,1)} %param.5) | copy-start | bytes 6291460
  25.6 23.1 %copy-start.1 = (bf16[1,2048,256]{2,1,0:T(8,128)(2,1)S(1)}, bf16[1,2048,256]{2,1,0:T(8,128)(2,1)}, u32[]{:S(2)}) copy-start(bf16[1,2048,256]{2,1,0:T(8,128)(2,1)} %param.8) | copy-start | bytes 3145732
  25.7 23.1 %copy-start.2 = (f32[1,16,4]{1,2,0:T(4,128)S(1)}, f32[1,16,4]{1,2,0:T(4,128)}, u32[]{:S(2)}) copy-start(f32[1,16,4]{1,2,0:T(4,128)} %param.6) | copy-start | bytes 772
  45.7 3.1 %collective-permute-start = (f32[16,64]{1,0:T(8,128)S(1)}, f32[16,64]{1,0:T(8,128)S(1)}, u32[]{:S(2)}, u32[]{:S(2)}) collective-permute-start(f32[16,64]{1,0:T(8,128)S(1)} %get-tuple-element.11), channel_id=1, source_target_pairs={{0,4},{4,0},{1,5},{5,1},{2,6},{6,2},{3,7},{7,3},{8,12},{12,8},{9,1... | collective-permute-start | bytes 12296 | tf_op jit(solution)/shard_map/ppermute | solution.py:236
  50.5 53.8 %copy-start.3 = (f32[256]{0:T(256)S(1)}, f32[256]{0:T(256)}, u32[]{:S(2)}) copy-start(f32[256]{0:T(256)} %param.9) | copy-start | bytes 3076

commit v5 on v4

--- a/solution.py
+++ b/solution.py
@@ -14,7 +14,6 @@
 LANES = 128
 PANEL = 32
 HALF = 16
-OUTER = 256
 
 
 forget_factor = 0.85
@@ -91,21 +90,20 @@
 
 def orthonormal_rows(work):
     size = work.shape[0]
-    for outer in range(0, size, OUTER):
-        end = min(outer + OUTER, size)
-        panel = work[outer : outer + PANEL, :]
-        for first in range(outer, end, PANEL):
-            second = first + PANEL
-            if second < end:
-                ahead = work[second : second + PANEL, :]
-                if first > outer:
-                    ahead = ahead - contract(work[outer:first, second : second + PANEL], work[outer:first, :], 0, 0)
-            rows = eliminate(panel, first)
-            work[first:second, :] = rows
-            if second < end:
-                panel = ahead - fold(rows, second)
-        if end < size:
-            work[end:, :] = work[end:, :] - contract(work[outer:end, end:size], work[outer:end, :], 0, 0)
+    panel = work[:PANEL, :]
+    for first in range(0, size, PANEL):
+        second = first + PANEL
+        left, later = first // LANES * LANES, second // LANES * LANES
+        if second < size:
+            ahead = work[second : second + PANEL, later:]
+            if first > 0:
+                ahead = ahead - contract(
+                    work[:first, second : second + PANEL], work[:first, later:], 0, 0
+                )
+        rows = eliminate(panel, first - left)
+        work[first:second, left:] = rows
+        if second < size:
+            panel = ahead - fold(rows[:, later - left :], second - later)
 
 
 def normalise(work):
@@ -163,6 +161,20 @@
         ),
         compiler_params=pltpu.CompilerParams(vmem_limit_bytes=8 * 2**20),
     )(incoming)
+
+
+def near_contract(a, b, a_dim, b_dim):
+    def halves(value):
+        high = value.astype(jnp.bfloat16)
+        return high, (value - high.astype(jnp.float32)).astype(jnp.bfloat16)
+
+    (a_high, a_low), (b_high, b_low) = halves(a), halves(b)
+    return lax.dot_general(
+        jnp.concatenate([a_high, a_high, a_low], axis=a_dim),
+        jnp.concatenate([b_high, b_low, b_high], axis=b_dim),
+        (((a_dim,), (b_dim,)), ((), ())),
+        preferred_element_type=jnp.float32,
+    )
 
 
 def rotate(
@@ -185,9 +197,11 @@
     work[:, size:] = contract(square, square, 1, 0)
     normalise(work)
     result = work[:, size:]
-    miss = contract(result, result, 1, 1) - jnp.where(row == column, 1.0, 0.0)
+    miss = near_contract(result, result, 1, 1) - jnp.where(row == column, 1.0, 0.0)
     half = jnp.where(row > column, miss, jnp.where(row == column, 0.5 * miss, 0.0))
-    rotation[...] = result - contract(half, result, 1, 0)
+    rotation[...] = result - jnp.dot(
+        half.astype(jnp.bfloat16), result.astype(jnp.bfloat16), preferred_element_type=jnp.float32
+    )
     sound = jnp.sum(miss * miss) < 1e-2
 
     @pl.when(jnp.logical_not(sound))
@@ -216,9 +230,9 @@
         copy = pltpu.make_async_copy(rows.at[span], rows_hbm.at[span], store.at[part])
         copy.start()
         storing.append(copy)
-    coords_ref[...] = contract(share_ref[...], turned, 1, 1)
-    energy = turned * contract(turned, gram[...], 1, 0)
-    total = contract(jnp.ones((8, size), jnp.float32), energy, 1, 1)
+    coords_ref[...] = near_contract(share_ref[...], turned, 1, 1)
+    energy = turned * near_contract(turned, gram[...], 1, 0)
+    total = near_contract(jnp.ones((16, size), jnp.float32), energy, 1, 1)
     singular_ref[...] = jnp.sqrt(total[:1])
     for copy in storing:
         copy.wait()

time: 147 us -> 146 us (level)
  no operation moved by 1% of the time
where the time goes in v5:
time: 146 us; the launch traced here: 145 us
  blocking collectives  53 us (36%)
  Pallas kernels  48.6 us (33%)
  starting transfers between devices  20.7 us (14%)
  waiting for transfers between devices  19.5 us (13%)
  local copies, waits for them, and re-layouts  2.43 us (2%)
    all_to_all x4, blocking collectives, all_to_all(): return lax.all_to_all(pieces, axes, 0, 0, tiled=True)  53 us
    pallas_call x1, Pallas kernels, finish(): pl.pallas_call(rotate, in_specs=[pl.BlockSpec(memory_space=pltpu.VMEM)] *...  40.9 us
    all_to_all x1, starting transfers between devices, all_to_all(): return lax.all_to_all(pieces, axes, 0, 0, tiled=True)  18.8 us
    all_to_all x1, waiting for transfers between devices, all_to_all(): return lax.all_to_all(pieces, axes, 0, 0, tiled=True)  18.3 us
    pallas_call x1, Pallas kernels, mass_pieces(): pl.pallas_call(functools.partial(mass_pieces_kernel, stored // steps), gr...  2.98 us
  transfers between devices with their start and end apart: 2, of which 2 were waited for; matrix products, arithmetic and copies ran while one was open for 1% of the time, Pallas kernels for 1%

profile of v5, /device:TPU:1, one launch (start us, length us, event | category | flops | bytes accessed | tf_op | source)
XLA Modules:
  0.0 145.4 jit_solution(9067677331947002496)
XLA Ops:
  0.6 3.0 %shard_map.76 = f32[1152,128]{1,0:T(8,128)} custom-call(bf16[2048,512]{1,0:T(8,128)(2,1)} %bitcast.15, f32[4,16]{1,0:T(4,128)} %bitcast.22, s32[1,16]{1,0:T(1,128)} %ids_ref.1), custom_call_target="tpu_custom_call" | custom-call | tf_op jit(solution)/shard_map/pallas_call | solution.py:324
  3.6 18.8 %all-to-all-start = ((f32[128,1,1152]{2,1,0:T(1,128)}), f32[128,1,1152]{2,1,0:T(1,128)}, u32[]{:S(2)}, u32[]{:S(2)}) async-start(f32[128,1,1152]{2,1,0:T(1,128)} %bitcast.25), calls=%async_computation | async-start | bytes 1179648 | tf_op jit(solution)/shard_map/all_to_all | solution.py:242
  22.4 0.7 slice.4.after_ref
  23.1 0.0 copy-start
  23.1 1.6 %copy-done = bf16[1,2048,512]{2,1,0:T(8,128)(2,1)S(1)} copy-done((bf16[1,2048,512]{2,1,0:T(8,128)(2,1)S(1)}, bf16[1,2048,512]{2,1,0:T(8,128)(2,1)}, u32[]{:S(2)}) %copy-start) | copy-done | bytes 2097176
  24.7 0.9 shard_map.77.before_ref.turned_ref
  25.6 0.0 copy-start.1
  25.7 0.0 copy-start.2
  25.7 0.1 pad_add_fusion.place_ref
  25.8 18.3 %all-to-all-done = f32[128,1,1152]{2,1,0:T(1,128)} async-done(((f32[128,1,1152]{2,1,0:T(1,128)}), f32[128,1,1152]{2,1,0:T(1,128)}, u32[]{:S(2)}, u32[]{:S(2)}) %all-to-all-start) | async-done | bytes 589856 | tf_op jit(solution)/shard_map/all_to_all | solution.py:242
  44.1 1.6 %shard_map.78 = (f32[16,64]{1,0:T(8,128)S(1)}, f32[16,64]{1,0:T(8,128)S(1)}) custom-call(s32[2]{0:T(128)S(1)} %pad_add_fusion.place_ref, f32[1152,128]{1,0:T(8,128)} %bitcast.6.incoming_ref, bf16[512,2048]{1,0:T(8,128)(2,1)S(1)} %shard_map.77.before_ref.turned_ref), custom_call_target="tpu_custom_call" | custom-call | tf_op jit(solution)/shard_map/pallas_call | solution.py:402
  45.7 1.9 %collective-permute-start = (f32[16,64]{1,0:T(8,128)S(1)}, f32[16,64]{1,0:T(8,128)S(1)}, u32[]{:S(2)}, u32[]{:S(2)}) collective-permute-start(f32[16,64]{1,0:T(8,128)S(1)} %get-tuple-element.11), channel_id=1, source_target_pairs={{0,4},{4,0},{1,5},{5,1},{2,6},{6,2},{3,7},{7,3},{8,12},{12,8},{9,1... | collective-permute-start | bytes 12296 | tf_op jit(solution)/shard_map/ppermute | solution.py:250
  47.6 1.1 collective-permute-done.come_ref
  48.8 0.0 copy-done.1
  48.8 0.0 copy-done.2
  48.8 1.7 %shard_map.79 = f32[512,256]{1,0:T(8,128)S(1)} custom-call(s32[1]{0:T(128)} %bitcast.core_ref, f32[16,64]{1,0:T(8,128)S(1)} %get-tuple-element.10.keep_ref, f32[16,64]{1,0:T(8,128)S(1)} %collective-permute-done.come_ref, f32[4,16]{1,0:T(4,128)S(1)} %bitcast.23, bf16[2048,256]{1,0:T(8,128)(2,1)S(1)} %bitcast.17, ...), custom_call_target="tpu_custom_call" | custom-call | tf_op jit(solution)/shard_map/pallas_call | solution.py:448
  50.5 0.0 copy-start.3
  50.5 13.0 %all_to_all.25.incoming_ref = f32[4,128,256]{2,1,0:T(8,128)S(1)} all-to-all(f32[4,128,256]{2,1,0:T(8,128)S(1)} %bitcast.19), channel_id=1, replica_groups=mesh['z'=8,'y'=8,'core'=2,'term'=4] {'term'}, dimensions={0} | all-to-all | bytes 1048576 | tf_op jit(solution)/shard_map/all_to_all | solution.py:242
  63.5 0.5 shard_map.80
  63.9 13.2 %all_to_all.26 = f32[32,1,1280]{2,1,0:T(1,128)S(1)} all-to-all(f32[32,1,1280]{2,1,0:T(1,128)S(1)} %bitcast.21), channel_id=1, replica_groups=mesh['z'=8,'y'=8,'core'=2,'term'=4] {'y','term'}, dimensions={0} | all-to-all | bytes 327680 | tf_op jit(solution)/shard_map/all_to_all | solution.py:242
  77.1 0.1 reduce_sum.18
  77.3 13.8 %all_to_all.27 = f32[16,1,1280]{2,1,0:T(1,128)S(1)} all-to-all(f32[16,1,1280]{2,1,0:T(1,128)S(1)} %broadcast_in_dim.6), channel_id=1, replica_groups=mesh['z'=8,'y'=8,'core'=2,'term'=4] {'z','core'}, dimensions={0} | all-to-all | bytes 163840 | tf_op jit(solution)/shard_map/all_to_all | solution.py:242
  91.1 0.1 reduce_sum.19
  91.1 0.1 broadcast_in_dim.7
  91.2 13.1 %all_to_all.28 = f32[32,1,1280]{2,1,0:T(1,128)S(1)} all-to-all(f32[32,1,1280]{2,1,0:T(1,128)S(1)} %broadcast_in_dim.7), channel_id=1, replica_groups=mesh['z'=8,'y'=8,'core'=2,'term'=4] {'y','term'}, dimensions={0} | all-to-all | bytes 327680 | tf_op jit(solution)/shard_map/all_to_all | solution.py:242
  104.3 0.0 copy-done.3
  104.3 40.9 %shard_map.81 = (f32[128,256]{1,0:T(8,128)}, bf16[2048,256]{1,0:T(8,128)(2,1)}, f32[1,256]{1,0:T(1,128)}) custom-call(f32[320,128]{1,0:T(8,128)S(1)} %bitcast.20, f32[1,256]{1,0:T(1,128)S(1)} %bitcast.24, f32[128,256]{1,0:T(8,128)S(1)} %get-tuple-element.13.share_ref, bf16[2048,256]{1,0:T(8,128)(2,1)S(1)} %bitcast.18), custom_call_target="tpu_custom_call" | custom-call | tf_op jit(solution)/shard_map/pallas_call | solution.py:256
  (1 shorter events, 0.0 us)
Async XLA Ops:
  3.6 40.5 %all-to-all-start = ((f32[128,1,1152]{2,1,0:T(1,128)}), f32[128,1,1152]{2,1,0:T(1,128)}, u32[]{:S(2)}, u32[]{:S(2)}) async-start(f32[128,1,1152]{2,1,0:T(1,128)} %bitcast.25), calls=%async_computation | async-start | bytes 1179648 | tf_op jit(solution)/shard_map/all_to_all | solution.py:242
  23.1 1.6 %copy-start = (bf16[1,2048,512]{2,1,0:T(8,128)(2,1)S(1)}, bf16[1,2048,512]{2,1,0:T(8,128)(2,1)}, u32[]{:S(2)}) copy-start(bf16[1,2048,512]{2,1,0:T(8,128)(2,1)} %param.5) | copy-start | bytes 6291460
  25.6 23.1 %copy-start.1 = (bf16[1,2048,256]{2,1,0:T(8,128)(2,1)S(1)}, bf16[1,2048,256]{2,1,0:T(8,128)(2,1)}, u32[]{:S(2)}) copy-start(bf16[1,2048,256]{2,1,0:T(8,128)(2,1)} %param.8) | copy-start | bytes 3145732
  25.7 23.1 %copy-start.2 = (f32[1,16,4]{1,2,0:T(4,128)S(1)}, f32[1,16,4]{1,2,0:T(4,128)}, u32[]{:S(2)}) copy-start(f32[1,16,4]{1,2,0:T(4,128)} %param.6) | copy-start | bytes 772
  45.7 3.1 %collective-permute-start = (f32[16,64]{1,0:T(8,128)S(1)}, f32[16,64]{1,0:T(8,128)S(1)}, u32[]{:S(2)}, u32[]{:S(2)}) collective-permute-start(f32[16,64]{1,0:T(8,128)S(1)} %get-tuple-element.11), channel_id=1, source_target_pairs={{0,4},{4,0},{1,5},{5,1},{2,6},{6,2},{3,7},{7,3},{8,12},{12,8},{9,1... | collective-permute-start | bytes 12296 | tf_op jit(solution)/shard_map/ppermute | solution.py:250
  50.5 53.8 %copy-start.3 = (f32[256]{0:T(256)S(1)}, f32[256]{0:T(256)}, u32[]{:S(2)}) copy-start(f32[256]{0:T(256)} %param.9) | copy-start | bytes 3076

commit v6 on v5

--- a/solution.py
+++ b/solution.py
@@ -247,7 +247,8 @@
 
 
 def swap_cores(array):
-    return lax.ppermute(array, "core", [(0, 1), (1, 0)])
+    both = lax.all_gather(array, "core", axis=0)
+    return jnp.where(lax.axis_index("core") == 0, both[1], both[0])
 
 
 def finish(packed, prior_sv, share_rows, basis_rows):

time: 146 us -> 145 us (level)
  starting transfers between devices: 20.7 us -> 18.8 us
  blocking collectives: 53 us -> 54.8 us
    ppermute x1 -> x0, starting transfers between devices: 1.92 us -> none  [swap_cores(): return lax.ppermute(array, 'core', [(0, 1), (1, 0)])]
    all_gather x0 -> x1, blocking collectives: none -> 1.81 us  [swap_cores(): both = lax.all_gather(array, 'core', axis=0)]
  transfers between devices with their start and end apart: 2 -> 1, of which waited for: 2 -> 1; matrix products, arithmetic and copies ran while one was open for 1% -> 1% of each run, Pallas kernels for 1% -> 1%
where the time goes in v6:
time: 145 us; the launch traced here: 144 us
  blocking collectives  54.8 us (38%)
  Pallas kernels  48.6 us (34%)
  starting transfers between devices  18.8 us (13%)
  waiting for transfers between devices  18.3 us (13%)
  local copies, waits for them, and re-layouts  2.43 us (2%)
    all_to_all x4, blocking collectives, all_to_all(): return lax.all_to_all(pieces, axes, 0, 0, tiled=True)  53 us
    pallas_call x1, Pallas kernels, finish(): pl.pallas_call(rotate, in_specs=[pl.BlockSpec(memory_space=pltpu.VMEM)] *...  40.9 us
    all_to_all x1, starting transfers between devices, all_to_all(): return lax.all_to_all(pieces, axes, 0, 0, tiled=True)  18.8 us
    all_to_all x1, waiting for transfers between devices, all_to_all(): return lax.all_to_all(pieces, axes, 0, 0, tiled=True)  18.3 us
    pallas_call x1, Pallas kernels, mass_pieces(): pl.pallas_call(functools.partial(mass_pieces_kernel, stored // steps), gr...  2.98 us
  transfers between devices with their start and end apart: 1, of which 1 were waited for; matrix products, arithmetic and copies ran while one was open for 1% of the time, Pallas kernels for 1%

profile of v6, /device:TPU:1, one launch (start us, length us, event | category | flops | bytes accessed | tf_op | source)
XLA Modules:
  0.0 144.2 jit_solution(4821487145331185605)
XLA Ops:
  0.6 3.0 %shard_map.76 = f32[1152,128]{1,0:T(8,128)} custom-call(bf16[2048,512]{1,0:T(8,128)(2,1)} %bitcast.15, f32[4,16]{1,0:T(4,128)} %bitcast.22, s32[1,16]{1,0:T(1,128)} %ids_ref.1), custom_call_target="tpu_custom_call" | custom-call | tf_op jit(solution)/shard_map/pallas_call | solution.py:325
  3.6 18.8 %all-to-all-start = ((f32[128,1,1152]{2,1,0:T(1,128)}), f32[128,1,1152]{2,1,0:T(1,128)}, u32[]{:S(2)}, u32[]{:S(2)}) async-start(f32[128,1,1152]{2,1,0:T(1,128)} %bitcast.25), calls=%async_computation | async-start | bytes 1179648 | tf_op jit(solution)/shard_map/all_to_all | solution.py:242
  22.4 0.7 slice.14.after_ref
  23.1 0.0 copy-start
  23.1 1.6 %copy-done = bf16[1,2048,512]{2,1,0:T(8,128)(2,1)S(1)} copy-done((bf16[1,2048,512]{2,1,0:T(8,128)(2,1)S(1)}, bf16[1,2048,512]{2,1,0:T(8,128)(2,1)}, u32[]{:S(2)}) %copy-start) | copy-done | bytes 2097176
  24.7 0.9 shard_map.77.before_ref.turned_ref
  25.6 0.0 copy-start.1
  25.7 0.0 copy-start.2
  25.7 0.1 pad_add_fusion.place_ref
  25.8 18.3 %all-to-all-done = f32[128,1,1152]{2,1,0:T(1,128)} async-done(((f32[128,1,1152]{2,1,0:T(1,128)}), f32[128,1,1152]{2,1,0:T(1,128)}, u32[]{:S(2)}, u32[]{:S(2)}) %all-to-all-start) | async-done | bytes 589856 | tf_op jit(solution)/shard_map/all_to_all | solution.py:242
  44.1 1.6 %shard_map.78 = (f32[16,64]{1,0:T(8,128)S(1)}, f32[16,64]{1,0:T(8,128)S(1)}) custom-call(s32[2]{0:T(128)S(1)} %pad_add_fusion.place_ref, f32[1152,128]{1,0:T(8,128)} %bitcast.6.incoming_ref, bf16[512,2048]{1,0:T(8,128)(2,1)S(1)} %shard_map.77.before_ref.turned_ref), custom_call_target="tpu_custom_call" | custom-call | tf_op jit(solution)/shard_map/pallas_call | solution.py:403
  45.7 1.8 %all-gather = f32[32,64]{1,0:T(8,128)S(1)} all-gather(f32[16,64]{1,0:T(8,128)S(1)} %get-tuple-element.11), channel_id=2, replica_groups=mesh['z'=8,'y'=8,'core'=2,'term'=4] {'core'}, dimensions={0}, use_global_device_ids=true | all-gather | bytes 12288 | tf_op jit(solution)/shard_map/all_gather | solution.py:250
  47.5 0.0 copy-done.1
  47.5 0.0 copy-done.2
  47.5 1.7 %shard_map.79 = f32[512,256]{1,0:T(8,128)S(1)} custom-call(s32[1]{0:T(128)} %bitcast.core_ref, f32[16,64]{1,0:T(8,128)S(1)} %get-tuple-element.10.keep_ref, f32[16,64]{1,0:T(8,128)S(1)} %slice_select_fusion.come_ref, f32[4,16]{1,0:T(4,128)S(1)} %bitcast.23, bf16[2048,256]{1,0:T(8,128)(2,1)S(1)} %bitcast.17, bf16[512,2048]{1,0:T(8,128)(2,1)S(1)} %shard_map.77.before_ref.turned_ref), custom_call_target="tpu_custom_call" | custom-call | tf_op jit(solution)/shard_map/pallas_call | solution.py:449
  49.3 0.0 copy-start.3
  49.3 12.9 %all_to_all.25.incoming_ref = f32[4,128,256]{2,1,0:T(8,128)S(1)} all-to-all(f32[4,128,256]{2,1,0:T(8,128)S(1)} %bitcast.19), channel_id=1, replica_groups=mesh['z'=8,'y'=8,'core'=2,'term'=4] {'term'}, dimensions={0} | all-to-all | bytes 1048576 | tf_op jit(solution)/shard_map/all_to_all | solution.py:242
  62.2 0.5 shard_map.80
  62.7 13.2 %all_to_all.26 = f32[32,1,1280]{2,1,0:T(1,128)S(1)} all-to-all(f32[32,1,1280]{2,1,0:T(1,128)S(1)} %bitcast.21), channel_id=1, replica_groups=mesh['z'=8,'y'=8,'core'=2,'term'=4] {'y','term'}, dimensions={0} | all-to-all | bytes 327680 | tf_op jit(solution)/shard_map/all_to_all | solution.py:242
  75.9 0.1 reduce_sum.18
  76.0 13.8 %all_to_all.27 = f32[16,1,1280]{2,1,0:T(1,128)S(1)} all-to-all(f32[16,1,1280]{2,1,0:T(1,128)S(1)} %broadcast_in_dim.6), channel_id=1, replica_groups=mesh['z'=8,'y'=8,'core'=2,'term'=4] {'z','core'}, dimensions={0} | all-to-all | bytes 163840 | tf_op jit(solution)/shard_map/all_to_all | solution.py:242
  89.8 0.1 reduce_sum.19
  89.9 0.1 broadcast_in_dim.7
  90.0 13.1 %all_to_all.28 = f32[32,1,1280]{2,1,0:T(1,128)S(1)} all-to-all(f32[32,1,1280]{2,1,0:T(1,128)S(1)} %broadcast_in_dim.7), channel_id=1, replica_groups=mesh['z'=8,'y'=8,'core'=2,'term'=4] {'y','term'}, dimensions={0} | all-to-all | bytes 327680 | tf_op jit(solution)/shard_map/all_to_all | solution.py:242
  103.1 0.0 copy-done.3
  103.1 40.9 %shard_map.81 = (f32[128,256]{1,0:T(8,128)}, bf16[2048,256]{1,0:T(8,128)(2,1)}, f32[1,256]{1,0:T(1,128)}) custom-call(f32[320,128]{1,0:T(8,128)S(1)} %bitcast.20, f32[1,256]{1,0:T(1,128)S(1)} %bitcast.24, f32[128,256]{1,0:T(8,128)S(1)} %get-tuple-element.13.share_ref, bf16[2048,256]{1,0:T(8,128)(2,1)S(1)} %bitcast.18), custom_call_target="tpu_custom_call" | custom-call | tf_op jit(solution)/shard_map/pallas_call | solution.py:257
  (2 shorter events, 0.0 us)
Async XLA Ops:
  3.6 40.5 %all-to-all-start = ((f32[128,1,1152]{2,1,0:T(1,128)}), f32[128,1,1152]{2,1,0:T(1,128)}, u32[]{:S(2)}, u32[]{:S(2)}) async-start(f32[128,1,1152]{2,1,0:T(1,128)} %bitcast.25), calls=%async_computation | async-start | bytes 1179648 | tf_op jit(solution)/shard_map/all_to_all | solution.py:242
  23.1 1.6 %copy-start = (bf16[1,2048,512]{2,1,0:T(8,128)(2,1)S(1)}, bf16[1,2048,512]{2,1,0:T(8,128)(2,1)}, u32[]{:S(2)}) copy-start(bf16[1,2048,512]{2,1,0:T(8,128)(2,1)} %param.5) | copy-start | bytes 6291460
  25.6 21.9 %copy-start.1 = (bf16[1,2048,256]{2,1,0:T(8,128)(2,1)S(1)}, bf16[1,2048,256]{2,1,0:T(8,128)(2,1)}, u32[]{:S(2)}) copy-start(bf16[1,2048,256]{2,1,0:T(8,128)(2,1)} %param.8) | copy-start | bytes 3145732
  25.7 21.9 %copy-start.2 = (f32[1,16,4]{1,2,0:T(4,128)S(1)}, f32[1,16,4]{1,2,0:T(4,128)}, u32[]{:S(2)}) copy-start(f32[1,16,4]{1,2,0:T(4,128)} %param.6) | copy-start | bytes 772
  49.3 53.8 %copy-start.3 = (f32[256]{0:T(256)S(1)}, f32[256]{0:T(256)}, u32[]{:S(2)}) copy-start(f32[256]{0:T(256)} %param.9) | copy-start | bytes 3076

commit v7 on v6

--- a/solution.py
+++ b/solution.py
@@ -353,7 +353,7 @@
         ],
         out_specs=pl.BlockSpec((docs, height // steps), lambda i: (0, i)),
         out_shape=jax.ShapeDtypeStruct((docs, height), counts.dtype),
-        compiler_params=pltpu.CompilerParams(vmem_limit_bytes=6 * 2**20),
+        compiler_params=pltpu.CompilerParams(vmem_limit_bytes=56 * 2**20),
         cost_estimate=pl.CostEstimate(
             flops=0, bytes_accessed=4 * height * docs, transcendentals=0
         ),
@@ -474,7 +474,7 @@
     turned = turn(counts, pieces[:8])
     chip = lax.axis_index("z") * lines + lax.axis_index("y")
     core = lax.axis_index("core")
-    keep, send = find_masses(incoming.reshape(-1, LANES), turned, chip, core, stored_blocks)
+    keep, send = find_masses(incoming.reshape(-1, LANES), turned[:16, :LANES], chip, core, stored_blocks)
     come = swap_cores(send)
     partial = project(core, keep, come, scales, basis_rows, turned, total_docs)
     partial = partial.reshape(term_count, share_docs, rank_size)

time: 145 us -> 146 us (level)
  Pallas kernels: 48.6 us -> 51.5 us
  waiting for transfers between devices: 18.3 us -> 15.6 us
    pallas_call x1, Pallas kernels: 0.92 us -> 4.3 us  [turn(): pl.pallas_call(turn_kernel, grid=(steps,), in_specs=[pl.BlockSpec(memory_...]
    all_to_all x1, waiting for transfers between devices: 18.3 us -> 15.6 us  [all_to_all(): return lax.all_to_all(pieces, axes, 0, 0, tiled=True)]
  transfers between devices with their start and end apart: 1 -> 1, of which waited for: 1 -> 1; matrix products, arithmetic and copies ran while one was open for 1% -> 1% of each run, Pallas kernels for 1% -> 3%
where the time goes in v7:
time: 146 us; the launch traced here: 145 us
  blocking collectives  54.8 us (38%)
  Pallas kernels  51.5 us (35%)
  starting transfers between devices  18.4 us (13%)
  waiting for transfers between devices  15.6 us (11%)
  local copies, waits for them, and re-layouts  3.68 us (3%)
    all_to_all x4, blocking collectives, all_to_all(): return lax.all_to_all(pieces, axes, 0, 0, tiled=True)  53 us
    pallas_call x1, Pallas kernels, finish(): pl.pallas_call(rotate, in_specs=[pl.BlockSpec(memory_space=pltpu.VMEM)] *...  40.9 us
    all_to_all x1, starting transfers between devices, all_to_all(): return lax.all_to_all(pieces, axes, 0, 0, tiled=True)  18.4 us
    all_to_all x1, waiting for transfers between devices, all_to_all(): return lax.all_to_all(pieces, axes, 0, 0, tiled=True)  15.6 us
    pallas_call x1, Pallas kernels, turn(): pl.pallas_call(turn_kernel, grid=(steps,), in_specs=[pl.BlockSpec(memory_...  4.3 us
    pallas_call x1, Pallas kernels, mass_pieces(): pl.pallas_call(functools.partial(mass_pieces_kernel, stored // steps), gr...  2.98 us
  transfers between devices with their start and end apart: 1, of which 1 were waited for; matrix products, arithmetic and copies ran while one was open for 1% of the time, Pallas kernels for 3%

profile of v7, /device:TPU:1, one launch (start us, length us, event | category | flops | bytes accessed | tf_op | source)
XLA Modules:
  0.0 145.1 jit_solution(18103946061939269298)
XLA Ops:
  0.6 3.0 %shard_map.76 = f32[1152,128]{1,0:T(8,128)} custom-call(bf16[2048,512]{1,0:T(8,128)(2,1)} %bitcast.24, f32[4,16]{1,0:T(4,128)} %bitcast.21, s32[1,16]{1,0:T(1,128)} %ids_ref.1), custom_call_target="tpu_custom_call" | custom-call | tf_op jit(solution)/shard_map/pallas_call | solution.py:325
  3.6 18.4 %all-to-all-start = ((f32[128,1,1152]{2,1,0:T(1,128)}), f32[128,1,1152]{2,1,0:T(1,128)S(1)}, u32[]{:S(2)}, u32[]{:S(2)}) async-start(f32[128,1,1152]{2,1,0:T(1,128)} %bitcast.26), calls=%async_computation | async-start | bytes 1179648 | tf_op jit(solution)/shard_map/all_to_all | solution.py:242
  22.0 1.3 slice.18.after_ref
  23.3 0.0 copy-start.1
  23.3 0.0 copy-start.2
  23.3 4.3 %shard_map.77.turned_ref = bf16[512,2048]{1,0:T(8,128)(2,1)} custom-call(f32[8,128]{1,0:T(8,128)} %slice.18.after_ref, bf16[2048,512]{1,0:T(8,128)(2,1)} %bitcast.25), custom_call_target="tpu_custom_call" | custom-call | bytes 4194304 | tf_op jit(solution)/shard_map/pallas_call | solution.py:347
  27.6 0.7 slice.19.before_ref
  28.3 0.1 pad_add_fusion.place_ref
  28.4 15.6 %all-to-all-done = f32[128,1,1152]{2,1,0:T(1,128)S(1)} async-done(((f32[128,1,1152]{2,1,0:T(1,128)}), f32[128,1,1152]{2,1,0:T(1,128)S(1)}, u32[]{:S(2)}, u32[]{:S(2)}) %all-to-all-start) | async-done | bytes 589856 | tf_op jit(solution)/shard_map/all_to_all | solution.py:242
  44.0 1.1 shard_map.78
  45.1 1.8 %all-gather = f32[32,64]{1,0:T(8,128)S(1)} all-gather(f32[16,64]{1,0:T(8,128)S(1)} %get-tuple-element.11), channel_id=2, replica_groups=mesh['z'=8,'y'=8,'core'=2,'term'=4] {'core'}, dimensions={0}, use_global_device_ids=true | all-gather | bytes 12288 | tf_op jit(solution)/shard_map/all_gather | solution.py:250
  46.9 0.0 copy-done.1
  46.9 0.0 copy-done.2
  46.9 0.0 copy-start
  46.9 1.6 %copy-done = bf16[512,2048]{1,0:T(8,128)(2,1)S(1)} copy-done((bf16[512,2048]{1,0:T(8,128)(2,1)S(1)}, bf16[512,2048]{1,0:T(8,128)(2,1)}, u32[]{:S(2)}) %copy-start) | copy-done | bytes 2097176
  48.5 1.7 %shard_map.79 = f32[512,256]{1,0:T(8,128)S(1)} custom-call(s32[1]{0:T(128)} %bitcast.core_ref, f32[16,64]{1,0:T(8,128)S(1)} %get-tuple-element.10.keep_ref, f32[16,64]{1,0:T(8,128)S(1)} %slice_select_fusion.come_ref, f32[4,16]{1,0:T(4,128)S(1)} %bitcast.22, bf16[2048,256]{1,0:T(8,128)(2,1)S(1)} %bitcast.15, bf16[512,2048]{1,0:T(8,128)(2,1)S(1)} %copy-done), custom_call_target="tpu_custom_call" | custom-call | tf_op jit(solution)/shard_map/pallas_call | solution.py:449
  50.2 0.0 copy-start.3
  50.2 12.9 %all_to_all.25.incoming_ref = f32[4,128,256]{2,1,0:T(8,128)S(1)} all-to-all(f32[4,128,256]{2,1,0:T(8,128)S(1)} %bitcast.18), channel_id=1, replica_groups=mesh['z'=8,'y'=8,'core'=2,'term'=4] {'term'}, dimensions={0} | all-to-all | bytes 1048576 | tf_op jit(solution)/shard_map/all_to_all | solution.py:242
  63.2 0.5 shard_map.80
  63.6 13.2 %all_to_all.26 = f32[32,1,1280]{2,1,0:T(1,128)S(1)} all-to-all(f32[32,1,1280]{2,1,0:T(1,128)S(1)} %bitcast.20), channel_id=1, replica_groups=mesh['z'=8,'y'=8,'core'=2,'term'=4] {'y','term'}, dimensions={0} | all-to-all | bytes 327680 | tf_op jit(solution)/shard_map/all_to_all | solution.py:242
  76.8 0.1 reduce_sum.18
  77.0 13.8 %all_to_all.27 = f32[16,1,1280]{2,1,0:T(1,128)S(1)} all-to-all(f32[16,1,1280]{2,1,0:T(1,128)S(1)} %broadcast_in_dim.6), channel_id=1, replica_groups=mesh['z'=8,'y'=8,'core'=2,'term'=4] {'z','core'}, dimensions={0} | all-to-all | bytes 163840 | tf_op jit(solution)/shard_map/all_to_all | solution.py:242
  90.8 0.1 reduce_sum.19
  90.8 0.1 broadcast_in_dim.7
  90.9 13.1 %all_to_all.28 = f32[32,1,1280]{2,1,0:T(1,128)S(1)} all-to-all(f32[32,1,1280]{2,1,0:T(1,128)S(1)} %broadcast_in_dim.7), channel_id=1, replica_groups=mesh['z'=8,'y'=8,'core'=2,'term'=4] {'y','term'}, dimensions={0} | all-to-all | bytes 327680 | tf_op jit(solution)/shard_map/all_to_all | solution.py:242
  104.0 0.0 copy-done.3
  104.0 40.9 %shard_map.81 = (f32[128,256]{1,0:T(8,128)}, bf16[2048,256]{1,0:T(8,128)(2,1)}, f32[1,256]{1,0:T(1,128)}) custom-call(f32[320,128]{1,0:T(8,128)S(1)} %bitcast.19, f32[1,256]{1,0:T(1,128)S(1)} %bitcast.23, f32[128,256]{1,0:T(8,128)S(1)} %get-tuple-element.13.share_ref, bf16[2048,256]{1,0:T(8,128)(2,1)S(1)} %bitcast.16), custom_call_target="tpu_custom_call" | custom-call | tf_op jit(solution)/shard_map/pallas_call | solution.py:257
  (2 shorter events, 0.0 us)
Async XLA Ops:
  3.6 40.4 %all-to-all-start = ((f32[128,1,1152]{2,1,0:T(1,128)}), f32[128,1,1152]{2,1,0:T(1,128)S(1)}, u32[]{:S(2)}, u32[]{:S(2)}) async-start(f32[128,1,1152]{2,1,0:T(1,128)} %bitcast.26), calls=%async_computation | async-start | bytes 1179648 | tf_op jit(solution)/shard_map/all_to_all | solution.py:242
  23.3 23.6 %copy-start.1 = (bf16[1,2048,256]{2,1,0:T(8,128)(2,1)S(1)}, bf16[1,2048,256]{2,1,0:T(8,128)(2,1)}, u32[]{:S(2)}) copy-start(bf16[1,2048,256]{2,1,0:T(8,128)(2,1)} %param.8) | copy-start | bytes 3145732
  23.3 23.6 %copy-start.2 = (f32[1,16,4]{1,2,0:T(4,128)S(1)}, f32[1,16,4]{1,2,0:T(4,128)}, u32[]{:S(2)}) copy-start(f32[1,16,4]{1,2,0:T(4,128)} %param.6) | copy-start | bytes 772
  46.9 1.6 %copy-start = (bf16[512,2048]{1,0:T(8,128)(2,1)S(1)}, bf16[512,2048]{1,0:T(8,128)(2,1)}, u32[]{:S(2)}) copy-start(bf16[512,2048]{1,0:T(8,128)(2,1)} %shard_map.77.turned_ref) | copy-start | bytes 6291460
  50.2 53.8 %copy-start.3 = (f32[256]{0:T(256)S(1)}, f32[256]{0:T(256)}, u32[]{:S(2)}) copy-start(f32[256]{0:T(256)} %param.9) | copy-start | bytes 3076
